TPU v7x, 256 devices: a whole 4x4x8 slice. The times are simulated.
256 devices in a mesh: down: 8 (over z), cross: 16 (over y, x), elev: 2 (over core).
Axes of the slice: x: 4, y: 4, z: 8, core: 2. Of those that a mesh axis runs over, the one named last changes fastest.
Arguments:
- source: float32 [256, 32, 256], P(('cross', 'elev'), 'down'), may hold values from -2 to 2
- pivot_inverse: bfloat16 [256, 32, 256, 256], P(('cross', 'elev'), 'down'), may hold values from -1.1 to 1.2
- coupling: bfloat16 [256, 32, 256, 256], P(('cross', 'elev'), 'down'), may hold values from -1.1 to 1.2
- skeleton_map: bfloat16 [256, 256, 256], P(('cross', 'elev')), may hold values from -0.375 to 0.375
- owners: int32 [256, 32], P(('cross', 'elev'), 'down'), may hold values from 0 to 255
Outputs:
- pressure: float32 [256, 32, 256], P(('cross', 'elev'), 'down')
- forces: float32 [256, 32, 256], P(('cross', 'elev'), 'down')
All inputs are finite; a program needn't handle non-finite values.
Results may differ from a plain program's by a relative error of at most 0.0003.
Values sent between devices are 32-bit elements; how exact they have to be, the bound alone decides.
No kernel may reach another device: no remote copies, remote signals or barrier semaphores. Data moves between devices by JAX's collectives and lax.ppermute only.
A program may use at most 128 MiB of HBM per device.

v0:
```python
import functools

import jax
import jax.numpy as jnp
from jax import lax
from jax.experimental import pallas as pl
from jax.experimental.pallas import tpu as pltpu
from jax.sharding import PartitionSpec as P

F32 = jnp.float32
BF16 = jnp.bfloat16
PLANE = ("cross", "elev")
MIB = 1024 * 1024
IN_VMEM = pl.BlockSpec(memory_space=pltpu.VMEM)
IN_HBM = pl.BlockSpec(memory_space=pltpu.HBM)
ANYWHERE = pl.BlockSpec(memory_space=pl.ANY)


def times(rows, matrix, transposed):
    return lax.dot_general(
        rows, matrix, (((1,), (1 if transposed else 0,)), ((), ())), preferred_element_type=F32
    )


def spread(vector):
    high = vector.astype(BF16).astype(F32)
    rest = vector - high
    middle = rest.astype(BF16).astype(F32)
    low = rest - middle
    parts = [high, middle, low]
    if vector.shape[0] % 16:
        parts.append(jnp.zeros_like(low))
    return jnp.concatenate(parts, axis=0).astype(BF16)


def per_line(vector, matrix_of, transposed, lines, twice=False):
    count = vector.shape[0]
    rows = spread(vector)
    if twice:
        rows = jnp.concatenate([rows, rows], axis=1)
    line_of = lax.rem(lax.broadcasted_iota(jnp.int32, vector.shape, 0), lines)
    total = jnp.zeros_like(vector)
    for line in range(lines):
        product = times(rows, matrix_of(line), transposed)
        product = product[:count] + product[count : 2 * count] + product[2 * count : 3 * count]
        total = jnp.where(line_of == line, product, total)
    return total


def halves(matrix):
    high = matrix.astype(BF16)
    low = (matrix - high.astype(F32)).astype(BF16)
    return jnp.concatenate([high, low], axis=1)


def product_of(pair, matrix, transposed):
    return times(pair, jnp.concatenate([matrix, matrix], axis=1 if transposed else 0), transposed)


def unit(size, sign=1.0):
    across = lax.broadcasted_iota(jnp.int32, (size, size), 0)
    along = lax.broadcasted_iota(jnp.int32, (size, size), 1)
    return jnp.where(across == along, sign, 0.0).astype(BF16)


def first_sweep(source, pivots, couple, leaving, pivots_here, couple_here, semaphores):
    lines, columns = source.shape[:2]

    @pl.when(lax.axis_index("down") == 0)
    def _():
        def fetch(column, far, near, kind):
            return pltpu.make_async_copy(far.at[:, column], near.at[:, column], semaphores.at[2 * column + kind])

        copies = [fetch(0, pivots, pivots_here, 1)]
        for column in range(1, columns):
            copies.append(fetch(column, couple, couple_here, 0))
            copies.append(fetch(column, pivots, pivots_here, 1))
        ahead = 4
        for copy in copies[:ahead]:
            copy.start()

        def take(at):
            copies[at].wait()
            if at + ahead < len(copies):
                copies[at + ahead].start()

        carried = None
        for column in range(columns):
            given = source[:, column, :]
            if column:
                take(2 * column - 1)
                given = given - per_line(carried, lambda l: couple_here[l, column], True, lines)
            take(2 * column)
            carried = per_line(given, lambda l: pivots_here[l, column], True, lines)
        leaving[...] = carried


EXTRA = 16
TOGETHER = 4


def store_pair(matrix, line, pair):
    size = matrix.shape[2]
    matrix[line, :size] = pair[:, :size]
    matrix[line, size:] = pair[:, size:]


def forward_rows(source, pivots, couple, lines, keep=None):
    columns, size = pivots.shape[1], pivots.shape[2]
    blank = jnp.zeros((EXTRA - 1, size), F32)
    values = None
    for column in range(columns):
        given = []
        for at, line in enumerate(lines):
            own = jnp.concatenate([source[line, pl.ds(column, 1), :], blank], axis=0)
            if column:
                sent = product_of(halves(values[at]), couple[line, column], True)
                given.append(jnp.concatenate([-sent[:size], own - sent[size:]], axis=0))
            else:
                given.append(jnp.concatenate([-times(unit(size), couple[line, 0], True), own], axis=0))
        values = [product_of(halves(x), pivots[l, column], True) for x, l in zip(given, lines)]
        if keep is not None and column < columns - 1:
            for at, value in enumerate(values):
                keep[at, column] = value
    return values


def transfer(source, pivots_far, couple_far, matrix, base, pivots, couple, kept, semaphores):
    lines, columns = pivots.shape[:2]
    size = pivots.shape[2]
    here = lax.axis_index("down")
    last = lax.axis_size("down") - 1

    def fetch(line, act):
        for kind, (far, near) in enumerate(((couple_far, couple), (pivots_far, pivots))):
            act(pltpu.make_async_copy(far.at[line], near.at[line], semaphores.at[kind, line]))

    def arrive(some, first):
        for line in some:
            fetch(line, lambda copy: copy.wait())

        @pl.when(first + TOGETHER < lines)
        def _():
            for line in some:
                fetch(line + TOGETHER, lambda copy: copy.start())

    def hand_over(some, values):
        for line, value in zip(some, values):
            store_pair(matrix, line, halves(value[:size]))
            base[pl.ds(line, 1), :] = value[size : size + 1]

    @pl.when(here > 0)
    def _():
        for line in range(TOGETHER):
            fetch(line, lambda copy: copy.start())

    @pl.when(jnp.logical_and(here > 0, here < last))
    def _():
        @pl.loop(0, lines, step=TOGETHER)
        def _(first):
            some = [first + k for k in range(TOGETHER)]
            arrive(some, first)
            hand_over(some, forward_rows(source, pivots, couple, some))

    @pl.when(here == last)
    def _():
        @pl.loop(0, lines, step=TOGETHER)
        def _(first):
            some = [first + k for k in range(TOGETHER)]
            arrive(some, first)
            values = forward_rows(source, pivots, couple, some, kept)
            for column in range(columns - 1, -1, -1):
                values = [product_of(halves(x), couple[l, column], False) for x, l in zip(values, some)]
                if column:
                    values = [
                        kept[at, column - 1] - product_of(halves(x), pivots[l, column - 1], True)
                        for at, (x, l) in enumerate(zip(values, some))
                    ]
            hand_over(some, values)


def reverse_transfer(pivots, couple, _, matrix):
    lines, columns = pivots.shape[:2]
    size = pivots.shape[2]
    here = lax.axis_index("down")
    last = lax.axis_size("down") - 1

    @pl.when(jnp.logical_and(here > 0, here < last))
    def _():
        @pl.loop(0, lines, step=TOGETHER)
        def _(first):
            some = [first + k for k in range(TOGETHER)]
            pairs = [times(unit(size, -1.0), pivots[l, columns - 1], True).astype(BF16) for l in some]
            for column in range(columns - 1, -1, -1):
                if column == columns - 1:
                    values = [times(x, couple[l, column], False) for x, l in zip(pairs, some)]
                else:
                    values = [product_of(x, couple[l, column], False) for x, l in zip(pairs, some)]
                pairs = [halves(value) for value in values]
                if column:
                    pairs = [halves(-product_of(x, pivots[l, column - 1], True)) for x, l in zip(pairs, some)]
            for line, pair in zip(some, pairs):
                store_pair(matrix, line, pair)


def step(place, arrived, matrix, base, _, out):
    lines = base.shape[0]

    @pl.when(lax.axis_index("down") == place)
    def _():
        out[...] = base[...] + per_line(arrived[...], lambda l: matrix[l], False, lines, twice=True)


def own_part(pivots, couple, source, arrived, _, forward, base):
    lines, columns = pivots.shape[:2]
    carried = jnp.sum(arrived[...], axis=0)
    for column in range(columns):
        given = source[:, column, :] - per_line(carried, lambda l: couple[l, column], True, lines)
        carried = per_line(given, lambda l: pivots[l, column], True, lines)
        forward[column] = carried
    value = carried
    for column in range(columns - 1, -1, -1):
        carried = per_line(value, lambda l: couple[l, column], False, lines)
        if column:
            value = forward[column - 1] - per_line(carried, lambda l: pivots[l, column - 1], True, lines)
    base[...] = carried


def finish(pivots, couple, skeleton, codes, forward, arrived, pressure, pushed):
    lines, columns = pivots.shape[:2]
    carried = jnp.sum(arrived[...], axis=0)
    values = [None] * columns
    for column in range(columns - 1, -1, -1):
        value = forward[column] - per_line(carried, lambda l: pivots[l, column], True, lines)
        values[column] = value
        pressure[:, column, :] = value
        if column:
            carried = per_line(value, lambda l: couple[l, column], False, lines)
    rows = columns * lines
    pushed[:rows] = per_line(jnp.concatenate(values, axis=0), lambda l: skeleton[l], True, lines)
    pushed[rows:] = codes[...]


def gather_rows(lines, columns, sides, *refs):
    blocks, outs = refs[: -sides], refs[-sides:]
    rows = lines * columns
    across, up = lax.axis_index("cross"), lax.axis_index("elev")
    width = blocks[0].shape[1]
    block_of = lax.broadcasted_iota(jnp.int32, (1, width), 1) // rows
    codes = jnp.zeros((1, width), F32)
    for at, block in enumerate(blocks):
        codes = jnp.where(block_of == at, block[rows : rows + 1, :], codes)
    values = jnp.concatenate([block[:rows, :] for block in blocks], axis=0)
    high = values.astype(BF16)
    rest = values - high.astype(F32)
    middle = rest.astype(BF16)
    low = (rest - middle.astype(F32)).astype(BF16)
    here = lax.broadcasted_iota(jnp.int32, (rows, 1), 0)
    wanted = []
    for way in range(sides):
        chip = (across // sides ^ way) * sides + lax.rem(across, sides)
        wanted.append((chip * 2 + up) * rows + here)
    wanted = jnp.concatenate(wanted, axis=0).astype(F32)
    chosen = jnp.where(wanted == codes, 1.0, 0.0).astype(BF16)
    total = times(chosen, high, False) + (times(chosen, middle, False) + times(chosen, low, False))
    for way in range(sides):
        outs[way][...] = total[way * rows : (way + 1) * rows]


def add_up(columns, *refs):
    parts, out = refs[:-1], refs[-1]
    total = parts[0][...]
    for part in parts[1:]:
        total = total + part[...]
    for row in range(out.shape[0]):
        out[row] = total[row * columns : (row + 1) * columns]


def call(body, out_shape, in_specs, scratch=(), name=None, limit=16):
    return pl.pallas_call(
        body,
        out_shape=out_shape,
        in_specs=in_specs,
        out_specs=jax.tree.map(lambda _: IN_VMEM, out_shape),
        scratch_shapes=list(scratch),
        compiler_params=pltpu.CompilerParams(vmem_limit_bytes=limit * MIB),
        name=name,
    )


def shaped(shape, dtype=F32):
    return jax.ShapeDtypeStruct(shape, dtype)


def shards(source, pivot_inverse, coupling, skeleton_map, owners):
    lines, columns, size = source.shape
    depth = lax.axis_size("down")
    vectors = shaped((lines, size))
    every = shaped((columns, lines, size))
    stacked = shaped((lines, 2 * size, size), BF16)

    matrices = pltpu.VMEM(pivot_inverse.shape, BF16)
    sent = call(
        first_sweep,
        vectors,
        [IN_VMEM, IN_HBM, IN_HBM],
        [matrices, matrices, pltpu.SemaphoreType.DMA((2 * columns,))],
        name="first_sweep",
        limit=51,
    )(source, pivot_inverse, coupling)
    arrivals = []
    base = matrix = back = None

    def advance(place, *operands):
        return call(
            functools.partial(step, place), vectors, [IN_VMEM, IN_VMEM, IN_VMEM, ANYWHERE], name="step"
        )(*operands)

    for hop in range(1, depth):
        arrived = lax.ppermute(sent, "down", [(hop - 1, hop)])
        arrivals.append(arrived)
        if hop == 1:
            matrix, base = call(
                transfer,
                (stacked, vectors),
                [IN_VMEM, IN_HBM, IN_HBM],
                [
                    matrices,
                    matrices,
                    pltpu.VMEM((TOGETHER, columns - 1, size + EXTRA, size), F32),
                    pltpu.SemaphoreType.DMA((2, lines)),
                ],
                name="transfer",
                limit=49,
            )(source, pivot_inverse, coupling)
        if hop == 4:
            back = call(
                reverse_transfer, stacked, [IN_VMEM, IN_VMEM, ANYWHERE], name="reverse_transfer"
            )(pivot_inverse, coupling, sent)
        sent = advance(hop, arrived, matrix, base, base if back is None else back)
    forward, base = call(
        own_part, (every, vectors), [IN_VMEM] * 4 + [ANYWHERE], name="own_part"
    )(pivot_inverse, coupling, source, jnp.stack(arrivals), sent)
    arrivals = []
    for hop in range(depth - 1, 0, -1):
        arrived = lax.ppermute(sent, "down", [(hop, hop - 1)])
        arrivals.append(arrived)
        if hop > 1:
            sent = advance(hop - 1, arrived, back, base, base)
    rows = lines * columns
    codes = (owners * columns + jnp.arange(columns, dtype=jnp.int32)).T.reshape(1, rows).astype(F32)
    codes = jnp.broadcast_to(jnp.tile(codes, (1, size // rows)), (8, size))
    pressure, own = call(
        finish, (shaped(source.shape), shaped((rows + 8, size))), [IN_VMEM] * 6, name="finish"
    )(pivot_inverse, coupling, skeleton_map, codes, forward, jnp.stack(arrivals))
    chips = lax.axis_size("cross")
    sides = 4
    blocks = [own]
    for way in range(1, sides):
        blocks.append(lax.ppermute(own, "cross", [(chip, chip ^ way) for chip in range(chips)]))
    blocks += [lax.ppermute(block, "elev", [(0, 1), (1, 0)]) for block in blocks]
    parts = call(
        functools.partial(gather_rows, lines, columns, sides),
        (shaped((rows, size)),) * sides,
        [IN_VMEM] * len(blocks),
        name="gather_rows",
    )(*blocks)
    parts = [
        lax.ppermute(part, "cross", [(chip, chip ^ sides * way) for chip in range(chips)]) if way else part
        for way, part in enumerate(parts)
    ]
    forces = call(
        functools.partial(add_up, columns), shaped(source.shape), [IN_VMEM] * sides, name="add_up"
    )(*parts)
    return (pressure, forces)


def solution(mesh):
    in_specs = (
        P(PLANE, "down", None),
        P(PLANE, "down", None, None),
        P(PLANE, "down", None, None),
        P(PLANE, None, None),
        P(PLANE, "down"),
    )
    out_specs = (P(PLANE, "down", None), P(PLANE, "down", None))
    return jax.shard_map(shards, mesh=mesh, in_specs=in_specs, out_specs=out_specs, check_vma=False)
```

profile of v0, /device:TPU:1, one launch (start us, length us, event | category | flops | bytes accessed | tf_op | source)
XLA Modules:
  0.0 95.3 jit_solution(550465785043254868)
XLA Ops:
  0.6 0.7 copy-done.4
  1.4 4.2 %first_sweep.1 = f32[8,256]{1,0:T(8,128)S(1)} custom-call(f32[8,4,256]{2,1,0:T(4,128)S(1)} %copy-done.4, bf16[8,4,256,256]{3,2,1,0:T(8,128)(2,1)} %pivots.7, bf16[8,4,256,256]{3,2,1,0:T(8,128)(2,1)} %couple.7), custom_call_target="tpu_custom_call" | custom-call | tf_op jit(solution)/shard_map/first_sweep/pallas_call | solution.py:303
  5.6 1.3 %collective-permute-start = (f32[8,256]{1,0:T(8,128)S(1)}, f32[8,256]{1,0:T(8,128)S(1)}, u32[]{:S(2)}, u32[]{:S(2)}) collective-permute-start(f32[8,256]{1,0:T(8,128)S(1)} %first_sweep.1), channel_id=1, source_target_pairs={{0,32},{1,33},{2,34},{3,35},{4,36},{5,37},{6,38},{7,39},{8,40},{9,... | collective-permute-start | bytes 24584 | tf_op jit(solution)/shard_map/ppermute | solution.py:320
  7.3 0.4 collective-permute-done.arrived
  7.7 0.8 collective-permute-start.1
  8.6 0.8 collective-permute-start.2
  9.4 0.7 collective-permute-start.3
  10.1 2.2 %copy-done.1 = bf16[8,4,256,256]{3,2,1,0:T(8,128)(2,1)S(1)} copy-done((bf16[8,4,256,256]{3,2,1,0:T(8,128)(2,1)S(1)}, bf16[8,4,256,256]{3,2,1,0:T(8,128)(2,1)}, u32[]{:S(2)}) %copy-start.1) | copy-done | bytes 4194328
  12.3 0.7 collective-permute-start.4
  13.0 0.7 collective-permute-start.5
  13.7 0.8 collective-permute-start.6
  14.8 0.8 collective-permute-start.7
  15.9 4.9 %own_part.1 = (f32[4,8,256]{2,1,0:T(8,128)S(1)}, f32[8,256]{1,0:T(8,128)S(1)}) custom-call(bf16[8,4,256,256]{3,2,1,0:T(8,128)(2,1)S(1)} %copy-done, bf16[8,4,256,256]{3,2,1,0:T(8,128)(2,1)S(1)} %copy-done.2, f32[8,4,256]{2,1,0:T(4,128)S(1)} %copy-done.5, f32[7,8,256]{2,1,0:T(8,128)S(1)} %constant_dynamic-update-slice_fusion.arrived, f32[8,256]{1,0:T(8,128)S(1)} %step.19._), custom_call_target="tpu_custom_call" | custom-call | tf_op jit(solution)/shard_map/own_part/pallas_call | solution.py:341
  20.8 0.7 collective-permute-start.8
  21.6 0.7 collective-permute-start.9
  22.3 0.8 collective-permute-start.10
  23.1 0.7 collective-permute-start.11
  23.8 0.7 collective-permute-start.12
  24.6 1.3 %collective-permute-start.13 = (f32[8,256]{1,0:T(8,128)S(1)}, f32[8,256]{1,0:T(8,128)S(1)}, u32[]{:S(2)}, u32[]{:S(2)}) collective-permute-start(f32[8,256]{1,0:T(8,128)S(1)} %step.25), channel_id=1, source_target_pairs={{32,0},{33,1},{34,2},{35,3},{36,4},{37,5},{38,6},{39,7},{40,8},{41... | collective-permute-start | bytes 24584 | tf_op jit(solution)/shard_map/ppermute | solution.py:346
  25.9 36.3 %collective-permute-done.13 = f32[8,256]{1,0:T(8,128)S(1)} collective-permute-done((f32[8,256]{1,0:T(8,128)S(1)}, f32[8,256]{1,0:T(8,128)S(1)}, u32[]{:S(2)}, u32[]{:S(2)}) %collective-permute-start.13) | collective-permute-done | bytes 8224 | tf_op jit(solution)/shard_map/ppermute | solution.py:346
  62.1 3.1 %finish.1 = (f32[8,4,256]{2,1,0:T(4,128)}, f32[40,256]{1,0:T(8,128)S(1)}) custom-call(bf16[8,4,256,256]{3,2,1,0:T(8,128)(2,1)S(1)} %copy-done, bf16[8,4,256,256]{3,2,1,0:T(8,128)(2,1)S(1)} %copy-done.2, bf16[8,256,256]{2,1,0:T(8,128)(2,1)S(1)} %copy-done.3, f32[8,256]{1,0:T(8,128)S(1)} %broadcast_in_dim.2.codes, f32[4,8,256]{2,1,0:T(8,128)S(1)} %get-tuple-element.14.forward, ...), custom_call_target="tpu_custom_call" | custom-call | tf_op jit(solution)/shard_map/finish/pallas_call | solution.py:353
  65.2 1.2 %collective-permute-start.14 = (f32[40,256]{1,0:T(8,128)S(1)}, f32[40,256]{1,0:T(8,128)S(1)}, u32[]{:S(2)}, u32[]{:S(2)}) collective-permute-start(f32[40,256]{1,0:T(8,128)S(1)} %get-tuple-element.17.refs_0_), channel_id=1, source_target_pairs={{0,2},{2,0},{4,6},{6,4},{8,10},{10,8},{12,14},{14,12},{16,18},{18,... | collective-permute-start | bytes 122888 | tf_op jit(solution)/shard_map/ppermute | solution.py:360
  66.5 2.5 %collective-permute-start.15 = (f32[40,256]{1,0:T(8,128)S(1)}, f32[40,256]{1,0:T(8,128)S(1)}, u32[]{:S(2)}, u32[]{:S(2)}) collective-permute-start(f32[40,256]{1,0:T(8,128)S(1)} %get-tuple-element.17.refs_0_), channel_id=1, source_target_pairs={{0,4},{2,6},{4,0},{6,2},{8,12},{10,14},{12,8},{14,10},{16,20},{18,... | collective-permute-start | bytes 122888 | tf_op jit(solution)/shard_map/ppermute | solution.py:360
  69.1 11.8 %collective-permute-start.17 = (f32[40,256]{1,0:T(8,128)S(1)}, f32[40,256]{1,0:T(8,128)S(1)}, u32[]{:S(2)}, u32[]{:S(2)}) collective-permute-start(f32[40,256]{1,0:T(8,128)S(1)} %get-tuple-element.17.refs_0_), channel_id=1, source_target_pairs={{0,1},{1,0},{2,3},{3,2},{4,5},{5,4},{6,7},{7,6},{8,9},{9,8},{10,11... | collective-permute-start | bytes 122888 | tf_op jit(solution)/shard_map/ppermute | solution.py:361
  80.9 2.3 %collective-permute-start.19 = (f32[40,256]{1,0:T(8,128)S(1)}, f32[40,256]{1,0:T(8,128)S(1)}, u32[]{:S(2)}, u32[]{:S(2)}) collective-permute-start(f32[40,256]{1,0:T(8,128)S(1)} %collective-permute-done.15.refs_2_), channel_id=1, source_target_pairs={{0,1},{1,0},{2,3},{3,2},{4,5},{5,4},{6,7},{7,6},{8,9},{9,8},{10,11... | collective-permute-start | bytes 122888 | tf_op jit(solution)/shard_map/ppermute | solution.py:361
  83.2 2.4 %collective-permute-start.20 = (f32[40,256]{1,0:T(8,128)S(1)}, f32[40,256]{1,0:T(8,128)S(1)}, u32[]{:S(2)}, u32[]{:S(2)}) collective-permute-start(f32[40,256]{1,0:T(8,128)S(1)} %collective-permute-done.16.refs_3_), channel_id=1, source_target_pairs={{0,1},{1,0},{2,3},{3,2},{4,5},{5,4},{6,7},{7,6},{8,9},{9,8},{10,11... | collective-permute-start | bytes 122888 | tf_op jit(solution)/shard_map/ppermute | solution.py:361
  85.6 0.9 collective-permute-done.20.refs_7_
  86.7 1.4 %collective-permute-start.21 = (f32[32,256]{1,0:T(8,128)S(1)}, f32[32,256]{1,0:T(8,128)S(1)}, u32[]{:S(2)}, u32[]{:S(2)}) collective-permute-start(f32[32,256]{1,0:T(8,128)S(1)} %get-tuple-element.19), channel_id=1, source_target_pairs={{0,8},{2,10},{4,12},{6,14},{8,0},{10,2},{12,4},{14,6},{16,24},{18,... | collective-permute-start | bytes 98312 | tf_op jit(solution)/shard_map/ppermute | solution.py:369
  88.1 2.6 %collective-permute-start.22 = (f32[32,256]{1,0:T(8,128)S(1)}, f32[32,256]{1,0:T(8,128)S(1)}, u32[]{:S(2)}, u32[]{:S(2)}) collective-permute-start(f32[32,256]{1,0:T(8,128)S(1)} %get-tuple-element.20), channel_id=1, source_target_pairs={{0,16},{2,18},{4,20},{6,22},{8,24},{10,26},{12,28},{14,30},{16,0},... | collective-permute-start | bytes 98312 | tf_op jit(solution)/shard_map/ppermute | solution.py:369
  90.7 1.6 %collective-permute-done.22.refs_2_ = f32[32,256]{1,0:T(8,128)S(1)} collective-permute-done((f32[32,256]{1,0:T(8,128)S(1)}, f32[32,256]{1,0:T(8,128)S(1)}, u32[]{:S(2)}, u32[]{:S(2)}) %collective-permute-start.22) | collective-permute-done | bytes 32800 | tf_op jit(solution)/shard_map/ppermute | solution.py:369
  92.4 2.3 %collective-permute-done.23.refs_3_ = f32[32,256]{1,0:T(8,128)S(1)} collective-permute-done((f32[32,256]{1,0:T(8,128)S(1)}, f32[32,256]{1,0:T(8,128)S(1)}, u32[]{:S(2)}, u32[]{:S(2)}) %collective-permute-start.23) | collective-permute-done | bytes 32800 | tf_op jit(solution)/shard_map/ppermute | solution.py:369
  94.7 0.6 add_up.1
  (69 shorter events, 1.6 us)
Async XLA Ops:
  0.6 0.8 copy-start.4
  1.4 5.6 %copy-start.6 = (s32[8,4]{0,1:T(4,128)S(1)}, s32[8,4]{0,1:T(4,128)}, u32[]{:S(2)}) copy-start(s32[8,4]{0,1:T(4,128)} %param.9) | copy-start | bytes 388
  5.6 2.1 %collective-permute-start = (f32[8,256]{1,0:T(8,128)S(1)}, f32[8,256]{1,0:T(8,128)S(1)}, u32[]{:S(2)}, u32[]{:S(2)}) collective-permute-start(f32[8,256]{1,0:T(8,128)S(1)} %first_sweep.1), channel_id=1, source_target_pairs={{0,32},{1,33},{2,34},{3,35},{4,36},{5,37},{6,38},{7,39},{8,40},{9,... | collective-permute-start | bytes 24584 | tf_op jit(solution)/shard_map/ppermute | solution.py:320
  7.3 2.8 %copy-start = (bf16[8,4,256,256]{3,2,1,0:T(8,128)(2,1)S(1)}, bf16[8,4,256,256]{3,2,1,0:T(8,128)(2,1)}, u32[]{:S(2)}) copy-start(bf16[8,4,256,256]{3,2,1,0:T(8,128)(2,1)} %pivots.7) | copy-start | bytes 12582916
  7.7 0.8 collective-permute-start.1
  8.6 0.8 collective-permute-start.2
  9.4 2.9 %collective-permute-start.3 = (f32[8,256]{1,0:T(8,128)S(1)}, f32[8,256]{1,0:T(8,128)S(1)}, u32[]{:S(2)}, u32[]{:S(2)}) collective-permute-start(f32[8,256]{1,0:T(8,128)S(1)} %step.15._), channel_id=1, source_target_pairs={{96,128},{97,129},{98,130},{99,131},{100,132},{101,133},{102,134},... | collective-permute-start | bytes 24584 | tf_op jit(solution)/shard_map/ppermute | solution.py:320
  10.1 2.2 %copy-start.1 = (bf16[8,4,256,256]{3,2,1,0:T(8,128)(2,1)S(1)}, bf16[8,4,256,256]{3,2,1,0:T(8,128)(2,1)}, u32[]{:S(2)}) copy-start(bf16[8,4,256,256]{3,2,1,0:T(8,128)(2,1)} %couple.7) | copy-start | bytes 12582916
  12.3 0.7 collective-permute-start.4
  13.0 0.7 collective-permute-start.5
  13.7 2.2 %copy-start.2 = (bf16[8,4,256,256]{3,2,1,0:T(8,128)(2,1)S(1)}, bf16[8,4,256,256]{3,2,1,0:T(8,128)(2,1)}, u32[]{:S(2)}) copy-start(bf16[8,4,256,256]{3,2,1,0:T(8,128)(2,1)} %couple.7) | copy-start | bytes 12582916
  13.7 2.2 %copy-start.5 = (f32[8,4,256]{2,1,0:T(4,128)S(1)}, f32[8,4,256]{2,1,0:T(4,128)}, u32[]{:S(2)}) copy-start(f32[8,4,256]{2,1,0:T(4,128)} %source.5) | copy-start | bytes 98308
  13.7 0.8 collective-permute-start.6
  14.8 6.0 %collective-permute-start.7 = (f32[8,256]{1,0:T(8,128)S(1)}, f32[8,256]{1,0:T(8,128)S(1)}, u32[]{:S(2)}, u32[]{:S(2)}) collective-permute-start(f32[8,256]{1,0:T(8,128)S(1)} %step.19._), channel_id=1, source_target_pairs={{224,192},{225,193},{226,194},{227,195},{228,196},{229,197},{230,1... | collective-permute-start | bytes 24584 | tf_op jit(solution)/shard_map/ppermute | solution.py:346
  20.8 0.7 collective-permute-start.8
  21.6 0.7 collective-permute-start.9
  22.2 39.9 %copy-start.3 = (bf16[8,256,256]{2,1,0:T(8,128)(2,1)S(1)}, bf16[8,256,256]{2,1,0:T(8,128)(2,1)}, u32[]{:S(2)}) copy-start(bf16[8,256,256]{2,1,0:T(8,128)(2,1)} %skeleton.1) | copy-start | bytes 3145732
  22.3 0.8 collective-permute-start.10
  23.1 0.7 collective-permute-start.11
  23.8 0.7 collective-permute-start.12
  24.6 37.6 %collective-permute-start.13 = (f32[8,256]{1,0:T(8,128)S(1)}, f32[8,256]{1,0:T(8,128)S(1)}, u32[]{:S(2)}, u32[]{:S(2)}) collective-permute-start(f32[8,256]{1,0:T(8,128)S(1)} %step.25), channel_id=1, source_target_pairs={{32,0},{33,1},{34,2},{35,3},{36,4},{37,5},{38,6},{39,7},{40,8},{41... | collective-permute-start | bytes 24584 | tf_op jit(solution)/shard_map/ppermute | solution.py:346
  65.2 15.6 %collective-permute-start.14 = (f32[40,256]{1,0:T(8,128)S(1)}, f32[40,256]{1,0:T(8,128)S(1)}, u32[]{:S(2)}, u32[]{:S(2)}) collective-permute-start(f32[40,256]{1,0:T(8,128)S(1)} %get-tuple-element.17.refs_0_), channel_id=1, source_target_pairs={{0,2},{2,0},{4,6},{6,4},{8,10},{10,8},{12,14},{14,12},{16,18},{18,... | collective-permute-start | bytes 122888 | tf_op jit(solution)/shard_map/ppermute | solution.py:360
  66.5 14.4 %collective-permute-start.15 = (f32[40,256]{1,0:T(8,128)S(1)}, f32[40,256]{1,0:T(8,128)S(1)}, u32[]{:S(2)}, u32[]{:S(2)}) collective-permute-start(f32[40,256]{1,0:T(8,128)S(1)} %get-tuple-element.17.refs_0_), channel_id=1, source_target_pairs={{0,4},{2,6},{4,0},{6,2},{8,12},{10,14},{12,8},{14,10},{16,20},{18,... | collective-permute-start | bytes 122888 | tf_op jit(solution)/shard_map/ppermute | solution.py:360
  68.9 14.2 %collective-permute-start.16 = (f32[40,256]{1,0:T(8,128)S(1)}, f32[40,256]{1,0:T(8,128)S(1)}, u32[]{:S(2)}, u32[]{:S(2)}) collective-permute-start(f32[40,256]{1,0:T(8,128)S(1)} %get-tuple-element.17.refs_0_), channel_id=1, source_target_pairs={{0,6},{2,4},{4,2},{6,0},{8,14},{10,12},{12,10},{14,8},{16,22},{18,... | collective-permute-start | bytes 122888 | tf_op jit(solution)/shard_map/ppermute | solution.py:360
  69.1 16.5 %collective-permute-start.17 = (f32[40,256]{1,0:T(8,128)S(1)}, f32[40,256]{1,0:T(8,128)S(1)}, u32[]{:S(2)}, u32[]{:S(2)}) collective-permute-start(f32[40,256]{1,0:T(8,128)S(1)} %get-tuple-element.17.refs_0_), channel_id=1, source_target_pairs={{0,1},{1,0},{2,3},{3,2},{4,5},{5,4},{6,7},{7,6},{8,9},{9,8},{10,11... | collective-permute-start | bytes 122888 | tf_op jit(solution)/shard_map/ppermute | solution.py:361
  80.9 4.7 %collective-permute-start.18 = (f32[40,256]{1,0:T(8,128)S(1)}, f32[40,256]{1,0:T(8,128)S(1)}, u32[]{:S(2)}, u32[]{:S(2)}) collective-permute-start(f32[40,256]{1,0:T(8,128)S(1)} %collective-permute-done.14.refs_1_), channel_id=1, source_target_pairs={{0,1},{1,0},{2,3},{3,2},{4,5},{5,4},{6,7},{7,6},{8,9},{9,8},{10,11... | collective-permute-start | bytes 122888 | tf_op jit(solution)/shard_map/ppermute | solution.py:361
  80.9 4.7 %collective-permute-start.19 = (f32[40,256]{1,0:T(8,128)S(1)}, f32[40,256]{1,0:T(8,128)S(1)}, u32[]{:S(2)}, u32[]{:S(2)}) collective-permute-start(f32[40,256]{1,0:T(8,128)S(1)} %collective-permute-done.15.refs_2_), channel_id=1, source_target_pairs={{0,1},{1,0},{2,3},{3,2},{4,5},{5,4},{6,7},{7,6},{8,9},{9,8},{10,11... | collective-permute-start | bytes 122888 | tf_op jit(solution)/shard_map/ppermute | solution.py:361
  83.2 3.3 %collective-permute-start.20 = (f32[40,256]{1,0:T(8,128)S(1)}, f32[40,256]{1,0:T(8,128)S(1)}, u32[]{:S(2)}, u32[]{:S(2)}) collective-permute-start(f32[40,256]{1,0:T(8,128)S(1)} %collective-permute-done.16.refs_3_), channel_id=1, source_target_pairs={{0,1},{1,0},{2,3},{3,2},{4,5},{5,4},{6,7},{7,6},{8,9},{9,8},{10,11... | collective-permute-start | bytes 122888 | tf_op jit(solution)/shard_map/ppermute | solution.py:361
  86.7 4.0 %collective-permute-start.21 = (f32[32,256]{1,0:T(8,128)S(1)}, f32[32,256]{1,0:T(8,128)S(1)}, u32[]{:S(2)}, u32[]{:S(2)}) collective-permute-start(f32[32,256]{1,0:T(8,128)S(1)} %get-tuple-element.19), channel_id=1, source_target_pairs={{0,8},{2,10},{4,12},{6,14},{8,0},{10,2},{12,4},{14,6},{16,24},{18,... | collective-permute-start | bytes 98312 | tf_op jit(solution)/shard_map/ppermute | solution.py:369
  88.1 4.3 %collective-permute-start.22 = (f32[32,256]{1,0:T(8,128)S(1)}, f32[32,256]{1,0:T(8,128)S(1)}, u32[]{:S(2)}, u32[]{:S(2)}) collective-permute-start(f32[32,256]{1,0:T(8,128)S(1)} %get-tuple-element.20), channel_id=1, source_target_pairs={{0,16},{2,18},{4,20},{6,22},{8,24},{10,26},{12,28},{14,30},{16,0},... | collective-permute-start | bytes 98312 | tf_op jit(solution)/shard_map/ppermute | solution.py:369
  90.7 4.0 %collective-permute-start.23 = (f32[32,256]{1,0:T(8,128)S(1)}, f32[32,256]{1,0:T(8,128)S(1)}, u32[]{:S(2)}, u32[]{:S(2)}) collective-permute-start(f32[32,256]{1,0:T(8,128)S(1)} %get-tuple-element.21), channel_id=1, source_target_pairs={{0,24},{2,26},{4,28},{6,30},{8,16},{10,18},{12,20},{14,22},{16,8},... | collective-permute-start | bytes 98312 | tf_op jit(solution)/shard_map/ppermute | solution.py:369
where the time goes:
time: 95.7 us; the launch traced here: 95.3 us
  waiting for transfers between devices  41.5 us (43%)
  starting transfers between devices  35.5 us (37%)
  Pallas kernels  13.7 us (14%)
  local copies, waits for them, and re-layouts  3.46 us (4%)
  between operations  1.13 us (1%)
    ppermute x7, waiting for transfers between devices, shards(): arrived = lax.ppermute(sent, 'down', [(hop, hop - 1)])  36.3 us
    ppermute x4, starting transfers between devices, shards(): lax.ppermute(block, 'elev', [(0, 1), (1, 0)])  16.5 us
    ppermute x7, starting transfers between devices, shards(): arrived = lax.ppermute(sent, 'down', [(hop - 1, hop)])  5.63 us
    ppermute x7, starting transfers between devices, shards(): arrived = lax.ppermute(sent, 'down', [(hop, hop - 1)])  5.52 us
    pallas_call x1, Pallas kernels, shards(): call(own_part, (every, vectors), [IN_VMEM] * 4 + [ANYWHERE], name='own_pa...  4.93 us
    pallas_call x1, Pallas kernels, shards(): call(first_sweep, vectors, [IN_VMEM, IN_HBM, IN_HBM], [matrices, matrices...  4.25 us
    ppermute x3, starting transfers between devices, shards(): lax.ppermute(part, 'cross', [(chip, chip ^ sides * way) for chip in range...  4.01 us
    ppermute x3, waiting for transfers between devices, shards(): lax.ppermute(part, 'cross', [(chip, chip ^ sides * way) for chip in range...  3.97 us
  transfers between devices with their start and end apart: 24, of which 5 were waited for; matrix products, arithmetic and copies ran while one was open for 0% of the time, Pallas kernels for 5%

commit v1 on v0

--- a/solution.py
+++ b/solution.py
@@ -63,7 +63,7 @@
     return jnp.where(across == along, sign, 0.0).astype(BF16)
 
 
-def first_sweep(source, pivots, couple, leaving, pivots_here, couple_here, semaphores):
+def first_sweep(source_far, pivots, couple, leaving, source, pivots_here, couple_here, semaphores):
     lines, columns = source.shape[:2]
 
     @pl.when(lax.axis_index("down") == 0)
@@ -76,8 +76,11 @@
             copies.append(fetch(column, couple, couple_here, 0))
             copies.append(fetch(column, pivots, pivots_here, 1))
         ahead = 4
+        given_copy = pltpu.make_async_copy(source_far, source, semaphores.at[0])
+        given_copy.start()
         for copy in copies[:ahead]:
             copy.start()
+        given_copy.wait()
 
         def take(at):
             copies[at].wait()
@@ -226,7 +229,7 @@
     base[...] = carried
 
 
-def finish(pivots, couple, skeleton, codes, forward, arrived, pressure, pushed):
+def finish(pivots, couple, skeleton, codes, slots, forward, arrived, _, pressure, pushed, packed):
     lines, columns = pivots.shape[:2]
     carried = jnp.sum(arrived[...], axis=0)
     values = [None] * columns
@@ -237,51 +240,125 @@
         if column:
             carried = per_line(value, lambda l: couple[l, column], False, lines)
     rows = columns * lines
-    pushed[:rows] = per_line(jnp.concatenate(values, axis=0), lambda l: skeleton[l], True, lines)
+    force = per_line(jnp.concatenate(values, axis=0), lambda l: skeleton[l], True, lines)
+    pushed[:rows] = force
     pushed[rows:] = codes[...]
-
-
-def gather_rows(lines, columns, sides, *refs):
-    blocks, outs = refs[: -sides], refs[-sides:]
+    slot = lax.broadcasted_iota(jnp.int32, (packed.shape[0], rows), 0).astype(F32)
+    chosen = jnp.where(slot == slots[:1, :rows], 1.0, 0.0).astype(BF16)
+    parts = spread(force)
+    packed[...] = times(chosen, parts[:rows], False) + (
+        times(chosen, parts[rows : 2 * rows], False) + times(chosen, parts[2 * rows :], False)
+    )
+
+
+def gather_rows(lines, columns, sides, own, pair, across, mine, theirs):
     rows = lines * columns
-    across, up = lax.axis_index("cross"), lax.axis_index("elev")
-    width = blocks[0].shape[1]
-    block_of = lax.broadcasted_iota(jnp.int32, (1, width), 1) // rows
-    codes = jnp.zeros((1, width), F32)
+    chip, core = lax.axis_index("cross"), lax.axis_index("elev")
+    height = own.shape[0]
+    blocks = [own[...], pair[:height], pair[height:], across[...]]
+    block_of = lax.broadcasted_iota(jnp.int32, (1, len(blocks) * rows), 1) // rows
+    codes = jnp.zeros(block_of.shape, F32)
     for at, block in enumerate(blocks):
-        codes = jnp.where(block_of == at, block[rows : rows + 1, :], codes)
-    values = jnp.concatenate([block[:rows, :] for block in blocks], axis=0)
+        codes = jnp.where(block_of == at, block[rows : rows + 1, : len(blocks) * rows], codes)
+    values = jnp.concatenate([block[:rows] for block in blocks], axis=0)
     high = values.astype(BF16)
     rest = values - high.astype(F32)
     middle = rest.astype(BF16)
     low = (rest - middle.astype(F32)).astype(BF16)
     here = lax.broadcasted_iota(jnp.int32, (rows, 1), 0)
     wanted = []
-    for way in range(sides):
-        chip = (across // sides ^ way) * sides + lax.rem(across, sides)
-        wanted.append((chip * 2 + up) * rows + here)
+    for turn in range(2):
+        holder = core if turn == 0 else 1 - core
+        beside = 1 + 2 * holder
+        for way, owner in ((0, holder), (2, holder), (beside, holder), (beside, 1 - holder)):
+            target = (chip // sides ^ way) * sides + lax.rem(chip, sides)
+            wanted.append((target * 2 + owner) * rows + here)
     wanted = jnp.concatenate(wanted, axis=0).astype(F32)
     chosen = jnp.where(wanted == codes, 1.0, 0.0).astype(BF16)
     total = times(chosen, high, False) + (times(chosen, middle, False) + times(chosen, low, False))
-    for way in range(sides):
-        outs[way][...] = total[way * rows : (way + 1) * rows]
-
-
-def add_up(columns, *refs):
-    parts, out = refs[:-1], refs[-1]
-    total = parts[0][...]
-    for part in parts[1:]:
-        total = total + part[...]
+    mine[...] = total[: 4 * rows]
+    theirs[...] = total[4 * rows :]
+
+
+def join(mine, other, own, across, pair):
+    rows = own.shape[0]
+    total = mine[...] + other[...]
+    own[...] = total[:rows]
+    across[...] = total[rows : 2 * rows]
+    pair[...] = total[2 * rows :]
+
+
+def add_near(own, across, pair, total, passed):
+    rows = own.shape[0]
+    total[...] = (own[...] + across[...]) + pair[:rows]
+    passed[...] = pair[rows:]
+
+
+def add_up(columns, near, other, out):
+    total = near[...] + other[...]
     for row in range(out.shape[0]):
         out[row] = total[row * columns : (row + 1) * columns]
 
 
-def call(body, out_shape, in_specs, scratch=(), name=None, limit=16):
+SLOTS = 8
+
+
+def announce(owners, _, out):
+    for device in range(out.shape[0]):
+        out[device] = owners[...]
+
+
+def plan_rows(lines, everyone, _, plan, crowded):
+    owner = everyone[:, 0, :]
+    devices, width = owner.shape
+    rows = plan.shape[1] // SLOTS
+    lane = lax.broadcasted_iota(jnp.int32, owner.shape, 1)
+    holder = jnp.where(lane < rows, jnp.floor(owner * (1.0 / lines)), -1.0)
+    rank = jnp.zeros(owner.shape, F32)
+    for row in range(rows):
+        same = jnp.logical_and(holder == holder[:, row : row + 1], lane > row)
+        rank = rank + jnp.where(same, 1.0, 0.0)
+    most = jnp.max(jnp.where(lane < rows, rank, 0.0))
+    crowded[0, 0] = jnp.where(most >= SLOTS, 1, 0).astype(jnp.int32)
+    me = (lax.axis_index("cross") * 2 + lax.axis_index("elev")).astype(F32)
+    columns = rows // lines
+    place = (owner - holder * lines) * columns + (lane // lines).astype(F32) + 1.0
+    place = jnp.where(holder == me, place, 0.0)
+    slots = jnp.zeros(owner.shape, F32)
+    for slot in range(SLOTS):
+        found = jnp.sum(jnp.where(rank == slot, place, 0.0), axis=1, keepdims=True)
+        slots = jnp.where(lane == slot, found, slots)
+    slot_of = lax.broadcasted_iota(jnp.int32, (width, plan.shape[1]), 0)
+    along = lax.broadcasted_iota(jnp.int32, (width, plan.shape[1]), 1)
+    repeat = jnp.where(slot_of == lax.rem(along, SLOTS), 1.0, 0.0).astype(BF16)
+    laid = times(slots.astype(BF16), repeat, False)
+    device = lax.broadcasted_iota(jnp.int32, laid.shape, 0)
+    wide = lax.broadcasted_iota(jnp.int32, laid.shape, 1)
+    plan[...] = jnp.broadcast_to(
+        jnp.sum(jnp.where(wide // SLOTS == device, laid, 0.0), axis=0, keepdims=True), plan.shape
+    )
+
+
+def place_rows(columns, plan, arrived, out):
+    rows = out.shape[0] * columns
+    values = arrived[...]
+    high = values.astype(BF16)
+    rest = values - high.astype(F32)
+    middle = rest.astype(BF16)
+    low = (rest - middle.astype(F32)).astype(BF16)
+    wanted = lax.broadcasted_iota(jnp.int32, (rows, values.shape[0]), 0).astype(F32) + 1.0
+    chosen = jnp.where(wanted == plan[:1], 1.0, 0.0).astype(BF16)
+    total = times(chosen, high, False) + (times(chosen, middle, False) + times(chosen, low, False))
+    for row in range(out.shape[0]):
+        out[row] = total[row * columns : (row + 1) * columns]
+
+
+def call(body, out_shape, in_specs, scratch=(), name=None, limit=16, out_specs=None):
     return pl.pallas_call(
         body,
         out_shape=out_shape,
         in_specs=in_specs,
-        out_specs=jax.tree.map(lambda _: IN_VMEM, out_shape),
+        out_specs=jax.tree.map(lambda _: IN_VMEM, out_shape) if out_specs is None else out_specs,
         scratch_shapes=list(scratch),
         compiler_params=pltpu.CompilerParams(vmem_limit_bytes=limit * MIB),
         name=name,
@@ -299,14 +376,67 @@
     every = shaped((columns, lines, size))
     stacked = shaped((lines, 2 * size, size), BF16)
 
+    group = lax.axis_size(PLANE)
+    rows = lines * columns
+    targets = owners.T.reshape(1, rows)
+    codes = (targets * columns + jnp.arange(rows, dtype=jnp.int32) // lines).astype(F32)
+    codes = jnp.broadcast_to(jnp.tile(codes, (1, size // rows)), (8, size))
+    holders = targets // lines
+    before = jnp.arange(rows)[:, None] < jnp.arange(rows)[None, :]
+    ranks = jnp.sum(jnp.logical_and(holders[0, :, None] == holders, before), axis=0, dtype=jnp.int32)
+    slots = jnp.where(ranks < SLOTS, holders * SLOTS + ranks, -1).astype(F32)
+    slots = jnp.broadcast_to(jnp.pad(slots, ((0, 0), (0, 128 - rows))), (8, 128))
+    announced = jnp.broadcast_to(jnp.pad(targets.astype(F32), ((0, 0), (0, 128 - rows))), (8, 128))
+
+    def dense(own, packed, plan):
+        chips = lax.axis_size("cross")
+        sides = 4
+
+        def other_core(block):
+            return lax.ppermute(block, "elev", [(0, 1), (1, 0)])
+
+        def across_ring(block, stride):
+            return lax.ppermute(block, "cross", [(chip, chip ^ 2 * stride) for chip in range(chips)])
+
+        def beside_ring(block, stride):
+            places = [(chip, core) for chip in range(chips) for core in range(2)]
+            return lax.ppermute(
+                block, PLANE, [(2 * chip + core, 2 * (chip ^ (1 + 2 * core) * stride) + core) for chip, core in places]
+            )
+
+        across = across_ring(own, 1)
+        pair = beside_ring(jnp.concatenate([own, other_core(own)], axis=0), 1)
+        quarter = shaped((rows, size))
+        mine, theirs = call(
+            functools.partial(gather_rows, lines, columns, sides),
+            (shaped((4 * rows, size)),) * 2,
+            [IN_VMEM] * 3,
+            name="gather_rows",
+        )(own, pair, across)
+        own, across, pair = call(
+            join, (quarter, quarter, shaped((2 * rows, size))), [IN_VMEM] * 2, name="join"
+        )(mine, other_core(theirs))
+        pair = beside_ring(pair, sides)
+        across = across_ring(across, sides)
+        near, passed = call(add_near, (quarter, quarter), [IN_VMEM] * 3, name="add_near")(own, across, pair)
+        return call(
+            functools.partial(add_up, columns), shaped(source.shape), [IN_VMEM] * 2, name="add_up"
+        )(near, other_core(passed))
+
+    def spread_out(own, packed, plan):
+        moved = lax.all_to_all(packed.reshape(group, SLOTS, size), PLANE, 0, 0)
+        return call(
+            functools.partial(place_rows, columns), shaped(source.shape), [IN_VMEM] * 2, name="place_rows"
+        )(plan, moved.reshape(group * SLOTS, size))
+
     matrices = pltpu.VMEM(pivot_inverse.shape, BF16)
     sent = call(
         first_sweep,
         vectors,
-        [IN_VMEM, IN_HBM, IN_HBM],
-        [matrices, matrices, pltpu.SemaphoreType.DMA((2 * columns,))],
+        [IN_HBM] * 3,
+        [pltpu.VMEM(source.shape, F32), matrices, matrices, pltpu.SemaphoreType.DMA((2 * columns,))],
         name="first_sweep",
-        limit=51,
+        limit=57,
     )(source, pivot_inverse, coupling)
     arrivals = []
     base = matrix = back = None
@@ -342,36 +472,30 @@
         own_part, (every, vectors), [IN_VMEM] * 4 + [ANYWHERE], name="own_part"
     )(pivot_inverse, coupling, source, jnp.stack(arrivals), sent)
     arrivals = []
+    everyone = None
     for hop in range(depth - 1, 0, -1):
         arrived = lax.ppermute(sent, "down", [(hop, hop - 1)])
         arrivals.append(arrived)
+        if hop == 2:
+            plan, crowded = call(
+                functools.partial(plan_rows, lines),
+                (shaped((8, group * SLOTS)), shaped((1, 1), jnp.int32)),
+                [IN_VMEM, ANYWHERE],
+                name="plan_rows",
+                out_specs=(IN_VMEM, pl.BlockSpec(memory_space=pltpu.SMEM)),
+            )(everyone, arrived)
+        if hop == depth - 4:
+            everyone = call(announce, shaped((group, 8, 128)), [IN_VMEM, ANYWHERE], name="announce")(announced, sent)
+            everyone = lax.all_to_all(everyone, PLANE, 0, 0)
         if hop > 1:
-            sent = advance(hop - 1, arrived, back, base, base)
-    rows = lines * columns
-    codes = (owners * columns + jnp.arange(columns, dtype=jnp.int32)).T.reshape(1, rows).astype(F32)
-    codes = jnp.broadcast_to(jnp.tile(codes, (1, size // rows)), (8, size))
-    pressure, own = call(
-        finish, (shaped(source.shape), shaped((rows + 8, size))), [IN_VMEM] * 6, name="finish"
-    )(pivot_inverse, coupling, skeleton_map, codes, forward, jnp.stack(arrivals))
-    chips = lax.axis_size("cross")
-    sides = 4
-    blocks = [own]
-    for way in range(1, sides):
-        blocks.append(lax.ppermute(own, "cross", [(chip, chip ^ way) for chip in range(chips)]))
-    blocks += [lax.ppermute(block, "elev", [(0, 1), (1, 0)]) for block in blocks]
-    parts = call(
-        functools.partial(gather_rows, lines, columns, sides),
-        (shaped((rows, size)),) * sides,
-        [IN_VMEM] * len(blocks),
-        name="gather_rows",
-    )(*blocks)
-    parts = [
-        lax.ppermute(part, "cross", [(chip, chip ^ sides * way) for chip in range(chips)]) if way else part
-        for way, part in enumerate(parts)
-    ]
-    forces = call(
-        functools.partial(add_up, columns), shaped(source.shape), [IN_VMEM] * sides, name="add_up"
-    )(*parts)
+            sent = advance(hop - 1, arrived, back, base, base if everyone is None else everyone)
+    pressure, own, packed = call(
+        finish,
+        (shaped(source.shape), shaped((rows + 8, size)), shaped((group * SLOTS, size))),
+        [IN_VMEM] * 7 + [ANYWHERE],
+        name="finish",
+    )(pivot_inverse, coupling, skeleton_map, codes, slots, forward, jnp.stack(arrivals), plan)
+    forces = lax.cond(crowded[0, 0] == 0, spread_out, dense, own, packed, plan)
     return (pressure, forces)
 
 

time: 95.7 us -> 96.1 us (level)
  blocking collectives: 0 us -> 20.1 us
  starting transfers between devices: 35.5 us -> 20.7 us
  waiting for transfers between devices: 41.5 us -> 30.4 us
  local copies, waits for them, and re-layouts: 3.46 us -> 7.34 us
  Pallas kernels: 13.7 us -> 15.2 us
    ppermute x10 -> x0, starting transfers between devices: 24.3 us -> none  [the longest x4 16.5 us: shards(): lax.ppermute(block, 'elev', [(0, 1), (1, 0)])]
    all_to_all x0 -> x1, blocking collectives: none -> 20.1 us  [spread_out(): moved = lax.all_to_all(packed.reshape(group, SLOTS, size), PLANE, 0, 0)]
    ppermute x7, waiting for transfers between devices: 36.3 us -> 22.4 us  [shards(): arrived = lax.ppermute(sent, 'down', [(hop, hop - 1)])]
    all_to_all x0 -> x1, starting transfers between devices: none -> 9.07 us  [shards(): everyone = lax.all_to_all(everyone, PLANE, 0, 0)]
    all_to_all x0 -> x1, waiting for transfers between devices: none -> 7.61 us  [shards(): everyone = lax.all_to_all(everyone, PLANE, 0, 0)]
    ppermute x10 -> x0, waiting for transfers between devices: 4.85 us -> none  [the longest x3 3.97 us: shards(): lax.ppermute(part, 'cross', [(chip, chip ^ sides * way) for chip in range...]
    unnamed x26 -> x34, local copies, waits for them, and re-layouts: 3.29 us -> 7.07 us
    pallas_call x4 -> x5, Pallas kernels: 8.24 us -> 9.97 us  [the longest x1 4.86 us: shards(): call(first_sweep, vectors, [IN_HBM] * 3, [pltpu.VMEM(source.shape, F32),...]
  transfers between devices with their start and end apart: 24 -> 15, of which waited for: 5 -> 3; matrix products, arithmetic and copies ran while one was open for 0% -> 0% of each run, Pallas kernels for 5% -> 7%
where the time goes in v1:
time: 96.1 us; the launch traced here: 95.7 us
  waiting for transfers between devices  30.4 us (32%)
  starting transfers between devices  20.7 us (22%)
  blocking collectives  20.1 us (21%)
  Pallas kernels  15.2 us (16%)
  local copies, waits for them, and re-layouts  7.34 us (8%)
  between operations  1.84 us (2%)
    ppermute x7, waiting for transfers between devices, shards(): arrived = lax.ppermute(sent, 'down', [(hop, hop - 1)])  22.4 us
    all_to_all x1, blocking collectives, spread_out(): moved = lax.all_to_all(packed.reshape(group, SLOTS, size), PLANE, 0, 0)  20.1 us
    all_to_all x1, starting transfers between devices, shards(): everyone = lax.all_to_all(everyone, PLANE, 0, 0)  9.07 us
    all_to_all x1, waiting for transfers between devices, shards(): everyone = lax.all_to_all(everyone, PLANE, 0, 0)  7.61 us
    unnamed x34, local copies, waits for them, and re-layouts  7.07 us
    ppermute x7, starting transfers between devices, shards(): arrived = lax.ppermute(sent, 'down', [(hop - 1, hop)])  5.81 us
    ppermute x7, starting transfers between devices, shards(): arrived = lax.ppermute(sent, 'down', [(hop, hop - 1)])  5.78 us
    pallas_call x1, Pallas kernels, shards(): call(own_part, (every, vectors), [IN_VMEM] * 4 + [ANYWHERE], name='own_pa...  4.93 us
  transfers between devices with their start and end apart: 15, of which 3 were waited for; matrix products, arithmetic and copies ran while one was open for 0% of the time, Pallas kernels for 7%

profile of v1, /device:TPU:1, one launch (start us, length us, event | category | flops | bytes accessed | tf_op | source)
XLA Modules:
  0.0 95.7 jit_solution(5346513420662596359)
XLA Ops:
  0.6 4.9 %first_sweep.1 = f32[8,256]{1,0:T(8,128)} custom-call(f32[8,4,256]{2,1,0:T(4,128)} %source.3, bf16[8,4,256,256]{3,2,1,0:T(8,128)(2,1)} %pivots.7, bf16[8,4,256,256]{3,2,1,0:T(8,128)(2,1)} %couple.7), custom_call_target="tpu_custom_call" | custom-call | tf_op jit(solution)/shard_map/first_sweep/pallas_call | solution.py:433
  5.5 1.3 %collective-permute-start.7 = (f32[8,256]{1,0:T(8,128)}, f32[8,256]{1,0:T(8,128)S(1)}, u32[]{:S(2)}, u32[]{:S(2)}) collective-permute-start(f32[8,256]{1,0:T(8,128)} %first_sweep.1), channel_id=1, source_target_pairs={{0,32},{1,33},{2,34},{3,35},{4,36},{5,37},{6,38},{7,39},{8,40},{9,... | collective-permute-start | bytes 24584 | tf_op jit(solution)/shard_map/ppermute | solution.py:450
  7.1 0.2 transfer.1
  7.4 0.4 collective-permute-done.7.arrived
  7.8 0.8 collective-permute-start.8
  8.6 0.8 collective-permute-start.9
  9.5 0.7 collective-permute-start.10
  10.3 2.2 %copy-done.2 = bf16[8,4,256,256]{3,2,1,0:T(8,128)(2,1)S(1)} copy-done((bf16[8,4,256,256]{3,2,1,0:T(8,128)(2,1)S(1)}, bf16[8,4,256,256]{3,2,1,0:T(8,128)(2,1)}, u32[]{:S(2)}) %copy-start.2) | copy-done | bytes 4194328
  12.5 1.6 %copy-done.6 = bf16[8,512,256]{2,1,0:T(8,128)(2,1)S(1)} copy-done((bf16[8,512,256]{2,1,0:T(8,128)(2,1)S(1)}, bf16[8,512,256]{2,1,0:T(8,128)(2,1)}, u32[]{:S(2)}) %copy-start.6) | copy-done | bytes 2097176
  14.1 0.6 collective-permute-start.11
  14.8 0.7 collective-permute-start.12
  15.5 1.0 %collective-permute-start.13 = (f32[8,256]{1,0:T(8,128)S(1)}, f32[8,256]{1,0:T(8,128)S(1)}, u32[]{:S(2)}, u32[]{:S(2)}) collective-permute-start(f32[8,256]{1,0:T(8,128)S(1)} %step.18), channel_id=1, source_target_pairs={{192,224},{193,225},{194,226},{195,227},{196,228},{197,229},{198,2... | collective-permute-start | bytes 24584 | tf_op jit(solution)/shard_map/ppermute | solution.py:450
  16.5 0.8 collective-permute-start.14
  17.3 0.3 copy-done.3
  17.6 4.9 %own_part.1 = (f32[4,8,256]{2,1,0:T(8,128)S(1)}, f32[8,256]{1,0:T(8,128)S(1)}) custom-call(bf16[8,4,256,256]{3,2,1,0:T(8,128)(2,1)S(1)} %copy-done, bf16[8,4,256,256]{3,2,1,0:T(8,128)(2,1)S(1)} %copy-done.3, f32[8,4,256]{2,1,0:T(4,128)S(1)} %copy-done.8, f32[7,8,256]{2,1,0:T(8,128)S(1)} %constant_dynamic-update-slice_fusion.arrived, f32[8,256]{1,0:T(8,128)S(1)} %step.19._), custom_call_target="tpu_custom_call" | custom-call | tf_op jit(solution)/shard_map/own_part/pallas_call | solution.py:471
  22.6 0.7 collective-permute-start.15
  23.3 0.7 collective-permute-start.16
  24.1 0.8 collective-permute-start.17
  24.9 0.7 announce.1
  25.5 9.1 %all-to-all-start.1 = ((f32[32,8,128]{2,1,0:T(8,128)}), f32[32,8,128]{2,1,0:T(8,128)S(1)}, u32[]{:S(2)}, u32[]{:S(2)}) async-start(f32[32,8,128]{2,1,0:T(8,128)} %announce.1), calls=%async_computation.1 | async-start | bytes 262144 | tf_op jit(solution)/shard_map/all_to_all | solution.py:489
  34.6 7.6 %all-to-all-done.1._.everyone = f32[32,8,128]{2,1,0:T(8,128)S(1)} async-done(((f32[32,8,128]{2,1,0:T(8,128)}), f32[32,8,128]{2,1,0:T(8,128)S(1)}, u32[]{:S(2)}, u32[]{:S(2)}) %all-to-all-start.1) | async-done | bytes 131104 | tf_op jit(solution)/shard_map/all_to_all | solution.py:489
  42.2 0.8 collective-permute-start.18
  43.1 0.8 collective-permute-start.19
  43.9 1.3 %collective-permute-start.20 = (f32[8,256]{1,0:T(8,128)S(1)}, f32[8,256]{1,0:T(8,128)S(1)}, u32[]{:S(2)}, u32[]{:S(2)}) collective-permute-start(f32[8,256]{1,0:T(8,128)S(1)} %step.25), channel_id=1, source_target_pairs={{32,0},{33,1},{34,2},{35,3},{36,4},{37,5},{38,6},{39,7},{40,8},{41... | collective-permute-start | bytes 24584 | tf_op jit(solution)/shard_map/ppermute | solution.py:477
  45.2 0.9 plan_rows.1
  46.8 22.4 %collective-permute-done.20 = f32[8,256]{1,0:T(8,128)S(1)} collective-permute-done((f32[8,256]{1,0:T(8,128)S(1)}, f32[8,256]{1,0:T(8,128)S(1)}, u32[]{:S(2)}, u32[]{:S(2)}) %collective-permute-start.20) | collective-permute-done | bytes 8224 | tf_op jit(solution)/shard_map/ppermute | solution.py:477
  69.2 2.2 %copy-done.4 = bf16[8,4,256,256]{3,2,1,0:T(8,128)(2,1)S(1)} copy-done((bf16[8,4,256,256]{3,2,1,0:T(8,128)(2,1)S(1)}, bf16[8,4,256,256]{3,2,1,0:T(8,128)(2,1)}, u32[]{:S(2)}) %copy-start.4) | copy-done | bytes 4194328
  71.4 3.3 %finish.1 = (f32[8,4,256]{2,1,0:T(4,128)}, f32[40,256]{1,0:T(8,128)S(1)}, f32[256,256]{1,0:T(8,128)S(1)}) custom-call(bf16[8,4,256,256]{3,2,1,0:T(8,128)(2,1)S(1)} %copy-done.1, bf16[8,4,256,256]{3,2,1,0:T(8,128)(2,1)S(1)} %copy-done.4, bf16[8,256,256]{2,1,0:T(8,128)(2,1)S(1)} %copy-done.7, f32[8,256]{1,0:T(8,128)S(1)} %broadcast_in_dim.14.codes, ...), custom_call_target="tpu_custom_call" | custom-call | tf_op jit(solution)/shard_map/finish/pallas_call | solution.py:492
  74.7 20.3 %conditional.1 = (f32[8,4,256]{2,1,0:T(4,128)S(1)}) conditional(s32[]{:T(128)} %bitcast.20, f32[40,256]{1,0:T(8,128)S(1)} %get-tuple-element.35, (f32[256,256]{1,0:T(8,128)S(1)}, f32[8,256]{1,0:T(8,128)S(1)}) %tuple.14), branch_computations={%region_1.2_spmd, %region_2.3_spmd} | conditional | flops 20480 | bytes 1868064 | solution.py:498
  74.7 20.1 %all_to_all.9 = f32[32,8,256]{2,1,0:T(8,128)S(1)} all-to-all(f32[32,8,256]{2,1,0:T(8,128)S(1)} %bitcast.42), channel_id=1, replica_groups=mesh['down'=8,'cross'=16,'elev'=2] {'cross','elev'}, dimensions={0} | all-to-all | bytes 524288 | tf_op jit(solution)/shard_map/cond/branch_1_fun/all_to_all | solution.py:427
  94.9 0.2 place_rows.1
  95.1 0.6 copy-done.9
  (69 shorter events, 0.8 us)
Async XLA Ops:
  0.6 6.5 %copy-start.8 = (f32[8,4,256]{2,1,0:T(4,128)S(1)}, f32[8,4,256]{2,1,0:T(4,128)}, u32[]{:S(2)}) copy-start(f32[8,4,256]{2,1,0:T(4,128)} %source.3) | copy-start | bytes 98308
  0.6 6.2 %copy-start.10 = (s32[8,4]{0,1:T(4,128)S(1)}, s32[8,4]{0,1:T(4,128)}, u32[]{:S(2)}) copy-start(s32[8,4]{0,1:T(4,128)} %param.11) | copy-start | bytes 388
  5.5 2.3 %collective-permute-start.7 = (f32[8,256]{1,0:T(8,128)}, f32[8,256]{1,0:T(8,128)S(1)}, u32[]{:S(2)}, u32[]{:S(2)}) collective-permute-start(f32[8,256]{1,0:T(8,128)} %first_sweep.1), channel_id=1, source_target_pairs={{0,32},{1,33},{2,34},{3,35},{4,36},{5,37},{6,38},{7,39},{8,40},{9,... | collective-permute-start | bytes 24584 | tf_op jit(solution)/shard_map/ppermute | solution.py:450
  7.3 2.8 %copy-start.5 = (bf16[8,512,256]{2,1,0:T(8,128)(2,1)}, bf16[8,512,256]{2,1,0:T(8,128)(2,1)S(1)}, u32[]{:S(2)}) copy-start(bf16[8,512,256]{2,1,0:T(8,128)(2,1)S(1)} %get-tuple-element.28.matrix) | copy-start | bytes 6291460
  7.4 2.9 %copy-start = (bf16[8,4,256,256]{3,2,1,0:T(8,128)(2,1)S(1)}, bf16[8,4,256,256]{3,2,1,0:T(8,128)(2,1)}, u32[]{:S(2)}) copy-start(bf16[8,4,256,256]{3,2,1,0:T(8,128)(2,1)} %pivots.7) | copy-start | bytes 12582916
  7.8 0.8 collective-permute-start.8
  8.6 0.8 collective-permute-start.9
  9.5 3.0 %collective-permute-start.10 = (f32[8,256]{1,0:T(8,128)S(1)}, f32[8,256]{1,0:T(8,128)S(1)}, u32[]{:S(2)}, u32[]{:S(2)}) collective-permute-start(f32[8,256]{1,0:T(8,128)S(1)} %step.15._), channel_id=1, source_target_pairs={{96,128},{97,129},{98,130},{99,131},{100,132},{101,133},{102,134},... | collective-permute-start | bytes 24584 | tf_op jit(solution)/shard_map/ppermute | solution.py:450
  10.3 2.2 %copy-start.2 = (bf16[8,4,256,256]{3,2,1,0:T(8,128)(2,1)S(1)}, bf16[8,4,256,256]{3,2,1,0:T(8,128)(2,1)}, u32[]{:S(2)}) copy-start(bf16[8,4,256,256]{3,2,1,0:T(8,128)(2,1)} %couple.7) | copy-start | bytes 12582916
  12.5 1.6 %copy-start.6 = (bf16[8,512,256]{2,1,0:T(8,128)(2,1)S(1)}, bf16[8,512,256]{2,1,0:T(8,128)(2,1)}, u32[]{:S(2)}) copy-start(bf16[8,512,256]{2,1,0:T(8,128)(2,1)} %copy-done.5) | copy-start | bytes 6291460
  14.1 0.7 collective-permute-start.11
  14.8 0.7 collective-permute-start.12
  15.5 2.2 %copy-start.3 = (bf16[8,4,256,256]{3,2,1,0:T(8,128)(2,1)S(1)}, bf16[8,4,256,256]{3,2,1,0:T(8,128)(2,1)}, u32[]{:S(2)}) copy-start(bf16[8,4,256,256]{3,2,1,0:T(8,128)(2,1)} %couple.7) | copy-start | bytes 12582916
  15.5 1.0 %collective-permute-start.13 = (f32[8,256]{1,0:T(8,128)S(1)}, f32[8,256]{1,0:T(8,128)S(1)}, u32[]{:S(2)}, u32[]{:S(2)}) collective-permute-start(f32[8,256]{1,0:T(8,128)S(1)} %step.18), channel_id=1, source_target_pairs={{192,224},{193,225},{194,226},{195,227},{196,228},{197,229},{198,2... | collective-permute-start | bytes 24584 | tf_op jit(solution)/shard_map/ppermute | solution.py:450
  16.5 6.0 %collective-permute-start.14 = (f32[8,256]{1,0:T(8,128)S(1)}, f32[8,256]{1,0:T(8,128)S(1)}, u32[]{:S(2)}, u32[]{:S(2)}) collective-permute-start(f32[8,256]{1,0:T(8,128)S(1)} %step.19._), channel_id=1, source_target_pairs={{224,192},{225,193},{226,194},{227,195},{228,196},{229,197},{230,1... | collective-permute-start | bytes 24584 | tf_op jit(solution)/shard_map/ppermute | solution.py:477
  22.6 0.7 collective-permute-start.15
  23.3 0.7 collective-permute-start.16
  24.0 45.2 %copy-start.7 = (bf16[8,256,256]{2,1,0:T(8,128)(2,1)S(1)}, bf16[8,256,256]{2,1,0:T(8,128)(2,1)}, u32[]{:S(2)}) copy-start(bf16[8,256,256]{2,1,0:T(8,128)(2,1)} %skeleton.1) | copy-start | bytes 3145732
  24.1 10.6 %collective-permute-start.17 = (f32[8,256]{1,0:T(8,128)S(1)}, f32[8,256]{1,0:T(8,128)S(1)}, u32[]{:S(2)}, u32[]{:S(2)}) collective-permute-start(f32[8,256]{1,0:T(8,128)S(1)} %step.22._), channel_id=1, source_target_pairs={{128,96},{129,97},{130,98},{131,99},{132,100},{133,101},{134,102},... | collective-permute-start | bytes 24584 | tf_op jit(solution)/shard_map/ppermute | solution.py:477
  25.5 16.7 %all-to-all-start.1 = ((f32[32,8,128]{2,1,0:T(8,128)}), f32[32,8,128]{2,1,0:T(8,128)S(1)}, u32[]{:S(2)}, u32[]{:S(2)}) async-start(f32[32,8,128]{2,1,0:T(8,128)} %announce.1), calls=%async_computation.1 | async-start | bytes 262144 | tf_op jit(solution)/shard_map/all_to_all | solution.py:489
  42.2 27.0 %copy-start.1 = (bf16[8,4,256,256]{3,2,1,0:T(8,128)(2,1)S(1)}, bf16[8,4,256,256]{3,2,1,0:T(8,128)(2,1)}, u32[]{:S(2)}) copy-start(bf16[8,4,256,256]{3,2,1,0:T(8,128)(2,1)} %pivots.7) | copy-start | bytes 12582916
  42.2 0.8 collective-permute-start.18
  43.1 0.8 collective-permute-start.19
  43.9 25.3 %collective-permute-start.20 = (f32[8,256]{1,0:T(8,128)S(1)}, f32[8,256]{1,0:T(8,128)S(1)}, u32[]{:S(2)}, u32[]{:S(2)}) collective-permute-start(f32[8,256]{1,0:T(8,128)S(1)} %step.25), channel_id=1, source_target_pairs={{32,0},{33,1},{34,2},{35,3},{36,4},{37,5},{38,6},{39,7},{40,8},{41... | collective-permute-start | bytes 24584 | tf_op jit(solution)/shard_map/ppermute | solution.py:477
  69.2 2.2 %copy-start.4 = (bf16[8,4,256,256]{3,2,1,0:T(8,128)(2,1)S(1)}, bf16[8,4,256,256]{3,2,1,0:T(8,128)(2,1)}, u32[]{:S(2)}) copy-start(bf16[8,4,256,256]{3,2,1,0:T(8,128)(2,1)} %couple.7) | copy-start | bytes 12582916
  95.1 0.6 copy-start.9

commit v2 on v1

--- a/solution.py
+++ b/solution.py
@@ -308,7 +308,8 @@
         out[device] = owners[...]
 
 
-def plan_rows(lines, everyone, _, plan, crowded):
+def plan_rows(lines, everyone, *refs):
+    plan, crowded = refs[-2:]
     owner = everyone[:, 0, :]
     devices, width = owner.shape
     rows = plan.shape[1] // SLOTS
@@ -476,19 +477,20 @@
     for hop in range(depth - 1, 0, -1):
         arrived = lax.ppermute(sent, "down", [(hop, hop - 1)])
         arrivals.append(arrived)
-        if hop == 2:
+        if hop == 3:
             plan, crowded = call(
                 functools.partial(plan_rows, lines),
                 (shaped((8, group * SLOTS)), shaped((1, 1), jnp.int32)),
-                [IN_VMEM, ANYWHERE],
+                [IN_VMEM] * 4 + [ANYWHERE],
                 name="plan_rows",
                 out_specs=(IN_VMEM, pl.BlockSpec(memory_space=pltpu.SMEM)),
-            )(everyone, arrived)
+            )(everyone, pivot_inverse, coupling, skeleton_map, arrived)
         if hop == depth - 4:
             everyone = call(announce, shaped((group, 8, 128)), [IN_VMEM, ANYWHERE], name="announce")(announced, sent)
             everyone = lax.all_to_all(everyone, PLANE, 0, 0)
         if hop > 1:
-            sent = advance(hop - 1, arrived, back, base, base if everyone is None else everyone)
+            ready = base if everyone is None else everyone if hop > 2 else plan
+            sent = advance(hop - 1, arrived, back, base, ready)
     pressure, own, packed = call(
         finish,
         (shaped(source.shape), shaped((rows + 8, size)), shaped((group * SLOTS, size))),

time: 96.1 us -> 93.8 us (0.976)
  waiting for transfers between devices: 30.4 us -> 27.4 us
    ppermute x7, waiting for transfers between devices: 22.4 us -> 19.4 us  [shards(): arrived = lax.ppermute(sent, 'down', [(hop, hop - 1)])]
    unnamed x34 -> x36, local copies, waits for them, and re-layouts: 7.07 us -> 7.6 us
where the time goes in v2:
time: 93.8 us; the launch traced here: 93.4 us
  waiting for transfers between devices  27.4 us (29%)
  starting transfers between devices  20.7 us (22%)
  blocking collectives  20 us (21%)
  Pallas kernels  15.2 us (16%)
  local copies, waits for them, and re-layouts  7.87 us (8%)
  between operations  2.14 us (2%)
    all_to_all x1, blocking collectives, spread_out(): moved = lax.all_to_all(packed.reshape(group, SLOTS, size), PLANE, 0, 0)  20 us
    ppermute x7, waiting for transfers between devices, shards(): arrived = lax.ppermute(sent, 'down', [(hop, hop - 1)])  19.4 us
    all_to_all x1, starting transfers between devices, shards(): everyone = lax.all_to_all(everyone, PLANE, 0, 0)  9.07 us
    all_to_all x1, waiting for transfers between devices, shards(): everyone = lax.all_to_all(everyone, PLANE, 0, 0)  7.61 us
    unnamed x36, local copies, waits for them, and re-layouts  7.6 us
    ppermute x7, starting transfers between devices, shards(): arrived = lax.ppermute(sent, 'down', [(hop - 1, hop)])  5.81 us
    ppermute x7, starting transfers between devices, shards(): arrived = lax.ppermute(sent, 'down', [(hop, hop - 1)])  5.78 us
    pallas_call x1, Pallas kernels, shards(): call(own_part, (every, vectors), [IN_VMEM] * 4 + [ANYWHERE], name='own_pa...  4.93 us
  transfers between devices with their start and end apart: 15, of which 3 were waited for; matrix products, arithmetic and copies ran while one was open for 0% of the time, Pallas kernels for 7%

profile of v2, /device:TPU:1, one launch (start us, length us, event | category | flops | bytes accessed | tf_op | source)
XLA Modules:
  0.0 93.4 jit_solution(5944824571187956306)
XLA Ops:
  0.6 4.9 %first_sweep.1 = f32[8,256]{1,0:T(8,128)} custom-call(f32[8,4,256]{2,1,0:T(4,128)} %source.3, bf16[8,4,256,256]{3,2,1,0:T(8,128)(2,1)} %pivots.7, bf16[8,4,256,256]{3,2,1,0:T(8,128)(2,1)} %couple.7), custom_call_target="tpu_custom_call" | custom-call | tf_op jit(solution)/shard_map/first_sweep/pallas_call | solution.py:434
  5.5 1.3 %collective-permute-start.7 = (f32[8,256]{1,0:T(8,128)}, f32[8,256]{1,0:T(8,128)S(1)}, u32[]{:S(2)}, u32[]{:S(2)}) collective-permute-start(f32[8,256]{1,0:T(8,128)} %first_sweep.1), channel_id=1, source_target_pairs={{0,32},{1,33},{2,34},{3,35},{4,36},{5,37},{6,38},{7,39},{8,40},{9,... | collective-permute-start | bytes 24584 | tf_op jit(solution)/shard_map/ppermute | solution.py:451
  7.4 0.4 collective-permute-done.7.arrived
  7.8 0.8 collective-permute-start.8
  8.6 0.8 collective-permute-start.9
  9.5 0.7 collective-permute-start.10
  10.3 2.2 %copy-done.2 = bf16[8,4,256,256]{3,2,1,0:T(8,128)(2,1)S(1)} copy-done((bf16[8,4,256,256]{3,2,1,0:T(8,128)(2,1)S(1)}, bf16[8,4,256,256]{3,2,1,0:T(8,128)(2,1)}, u32[]{:S(2)}) %copy-start.2) | copy-done | bytes 4194328
  12.5 1.6 %copy-done.7 = bf16[8,512,256]{2,1,0:T(8,128)(2,1)S(1)} copy-done((bf16[8,512,256]{2,1,0:T(8,128)(2,1)S(1)}, bf16[8,512,256]{2,1,0:T(8,128)(2,1)}, u32[]{:S(2)}) %copy-start.7) | copy-done | bytes 2097176
  14.1 0.6 collective-permute-start.11
  14.8 0.7 collective-permute-start.12
  15.5 1.0 %collective-permute-start.13 = (f32[8,256]{1,0:T(8,128)S(1)}, f32[8,256]{1,0:T(8,128)S(1)}, u32[]{:S(2)}, u32[]{:S(2)}) collective-permute-start(f32[8,256]{1,0:T(8,128)S(1)} %step.18), channel_id=1, source_target_pairs={{192,224},{193,225},{194,226},{195,227},{196,228},{197,229},{198,2... | collective-permute-start | bytes 24584 | tf_op jit(solution)/shard_map/ppermute | solution.py:451
  16.5 0.8 collective-permute-start.14
  17.3 0.3 copy-done.3
  17.6 4.9 %own_part.1 = (f32[4,8,256]{2,1,0:T(8,128)S(1)}, f32[8,256]{1,0:T(8,128)S(1)}) custom-call(bf16[8,4,256,256]{3,2,1,0:T(8,128)(2,1)S(1)} %copy-done, bf16[8,4,256,256]{3,2,1,0:T(8,128)(2,1)S(1)} %copy-done.3, f32[8,4,256]{2,1,0:T(4,128)S(1)} %copy-done.9, f32[7,8,256]{2,1,0:T(8,128)S(1)} %constant_dynamic-update-slice_fusion.arrived, f32[8,256]{1,0:T(8,128)S(1)} %step.19._), custom_call_target="tpu_custom_call" | custom-call | tf_op jit(solution)/shard_map/own_part/pallas_call | solution.py:472
  22.6 0.7 collective-permute-start.15
  23.3 0.8 collective-permute-start.16
  24.2 0.7 collective-permute-start.17
  24.9 0.7 announce.1
  25.5 9.1 %all-to-all-start.1 = ((f32[32,8,128]{2,1,0:T(8,128)}), f32[32,8,128]{2,1,0:T(8,128)S(1)}, u32[]{:S(2)}, u32[]{:S(2)}) async-start(f32[32,8,128]{2,1,0:T(8,128)} %announce.1), calls=%async_computation.1 | async-start | bytes 262144 | tf_op jit(solution)/shard_map/all_to_all | solution.py:490
  34.6 7.6 %all-to-all-done.1._.everyone = f32[32,8,128]{2,1,0:T(8,128)S(1)} async-done(((f32[32,8,128]{2,1,0:T(8,128)}), f32[32,8,128]{2,1,0:T(8,128)S(1)}, u32[]{:S(2)}, u32[]{:S(2)}) %all-to-all-start.1) | async-done | bytes 131104 | tf_op jit(solution)/shard_map/all_to_all | solution.py:490
  42.2 0.8 collective-permute-start.18
  43.1 0.8 collective-permute-start.19
  43.9 0.5 copy-done.1
  44.4 2.2 %copy-done.4 = bf16[8,4,256,256]{3,2,1,0:T(8,128)(2,1)S(1)} copy-done((bf16[8,4,256,256]{3,2,1,0:T(8,128)(2,1)S(1)}, bf16[8,4,256,256]{3,2,1,0:T(8,128)(2,1)}, u32[]{:S(2)}) %copy-start.4) | copy-done | bytes 4194328
  46.6 0.9 %plan_rows.1 = (f32[8,256]{1,0:T(8,128)S(1)}, s32[1,1]{1,0:T(1,128)}) custom-call(f32[32,8,128]{2,1,0:T(8,128)S(1)} %all-to-all-done.1._.everyone, bf16[8,4,256,256]{3,2,1,0:T(8,128)(2,1)S(1)} %copy-done.1, bf16[8,4,256,256]{3,2,1,0:T(8,128)(2,1)S(1)} %copy-done.4, bf16[8,256,256]{2,1,0:T(8,128)(2,1)S(1)} %copy-done.8, ...), custom_call_target="tpu_custom_call" | custom-call | tf_op jit(solution)/shard_map/plan_rows/pallas_call | solution.py:481
  48.6 1.3 %collective-permute-start.20 = (f32[8,256]{1,0:T(8,128)S(1)}, f32[8,256]{1,0:T(8,128)S(1)}, u32[]{:S(2)}, u32[]{:S(2)}) collective-permute-start(f32[8,256]{1,0:T(8,128)S(1)} %step.25), channel_id=1, source_target_pairs={{32,0},{33,1},{34,2},{35,3},{36,4},{37,5},{38,6},{39,7},{40,8},{41... | collective-permute-start | bytes 24584 | tf_op jit(solution)/shard_map/ppermute | solution.py:478
  49.9 19.3 %collective-permute-done.20 = f32[8,256]{1,0:T(8,128)S(1)} collective-permute-done((f32[8,256]{1,0:T(8,128)S(1)}, f32[8,256]{1,0:T(8,128)S(1)}, u32[]{:S(2)}, u32[]{:S(2)}) %collective-permute-start.20) | collective-permute-done | bytes 8224 | tf_op jit(solution)/shard_map/ppermute | solution.py:478
  69.2 3.3 %finish.1 = (f32[8,4,256]{2,1,0:T(4,128)}, f32[40,256]{1,0:T(8,128)S(1)}, f32[256,256]{1,0:T(8,128)S(1)}) custom-call(bf16[8,4,256,256]{3,2,1,0:T(8,128)(2,1)S(1)} %copy-done.1, bf16[8,4,256,256]{3,2,1,0:T(8,128)(2,1)S(1)} %copy-done.5, bf16[8,256,256]{2,1,0:T(8,128)(2,1)S(1)} %copy-done.8, f32[8,256]{1,0:T(8,128)S(1)} %broadcast_in_dim.14.codes, ...), custom_call_target="tpu_custom_call" | custom-call | tf_op jit(solution)/shard_map/finish/pallas_call | solution.py:494
  72.5 20.2 %conditional.1 = (f32[8,4,256]{2,1,0:T(4,128)S(1)}) conditional(s32[]{:T(128)} %bitcast.20, f32[40,256]{1,0:T(8,128)S(1)} %get-tuple-element.35, (f32[256,256]{1,0:T(8,128)S(1)}, f32[8,256]{1,0:T(8,128)S(1)}) %tuple.14), branch_computations={%region_1.2_spmd, %region_2.3_spmd} | conditional | flops 20480 | bytes 1868064 | solution.py:500
  72.5 20.0 %all_to_all.9 = f32[32,8,256]{2,1,0:T(8,128)S(1)} all-to-all(f32[32,8,256]{2,1,0:T(8,128)S(1)} %bitcast.42), channel_id=1, replica_groups=mesh['down'=8,'cross'=16,'elev'=2] {'cross','elev'}, dimensions={0} | all-to-all | bytes 524288 | tf_op jit(solution)/shard_map/cond/branch_1_fun/all_to_all | solution.py:428
  92.5 0.2 place_rows.1
  92.7 0.6 copy-done.10
  (71 shorter events, 0.9 us)
Async XLA Ops:
  0.6 6.5 %copy-start.9 = (f32[8,4,256]{2,1,0:T(4,128)S(1)}, f32[8,4,256]{2,1,0:T(4,128)}, u32[]{:S(2)}) copy-start(f32[8,4,256]{2,1,0:T(4,128)} %source.3) | copy-start | bytes 98308
  0.6 6.2 %copy-start.11 = (s32[8,4]{0,1:T(4,128)S(1)}, s32[8,4]{0,1:T(4,128)}, u32[]{:S(2)}) copy-start(s32[8,4]{0,1:T(4,128)} %param.11) | copy-start | bytes 388
  5.5 2.3 %collective-permute-start.7 = (f32[8,256]{1,0:T(8,128)}, f32[8,256]{1,0:T(8,128)S(1)}, u32[]{:S(2)}, u32[]{:S(2)}) collective-permute-start(f32[8,256]{1,0:T(8,128)} %first_sweep.1), channel_id=1, source_target_pairs={{0,32},{1,33},{2,34},{3,35},{4,36},{5,37},{6,38},{7,39},{8,40},{9,... | collective-permute-start | bytes 24584 | tf_op jit(solution)/shard_map/ppermute | solution.py:451
  7.3 2.8 %copy-start.6 = (bf16[8,512,256]{2,1,0:T(8,128)(2,1)}, bf16[8,512,256]{2,1,0:T(8,128)(2,1)S(1)}, u32[]{:S(2)}) copy-start(bf16[8,512,256]{2,1,0:T(8,128)(2,1)S(1)} %get-tuple-element.28.matrix) | copy-start | bytes 6291460
  7.4 2.9 %copy-start = (bf16[8,4,256,256]{3,2,1,0:T(8,128)(2,1)S(1)}, bf16[8,4,256,256]{3,2,1,0:T(8,128)(2,1)}, u32[]{:S(2)}) copy-start(bf16[8,4,256,256]{3,2,1,0:T(8,128)(2,1)} %pivots.7) | copy-start | bytes 12582916
  7.8 0.8 collective-permute-start.8
  8.6 0.8 collective-permute-start.9
  9.5 3.0 %collective-permute-start.10 = (f32[8,256]{1,0:T(8,128)S(1)}, f32[8,256]{1,0:T(8,128)S(1)}, u32[]{:S(2)}, u32[]{:S(2)}) collective-permute-start(f32[8,256]{1,0:T(8,128)S(1)} %step.15._), channel_id=1, source_target_pairs={{96,128},{97,129},{98,130},{99,131},{100,132},{101,133},{102,134},... | collective-permute-start | bytes 24584 | tf_op jit(solution)/shard_map/ppermute | solution.py:451
  10.3 2.2 %copy-start.2 = (bf16[8,4,256,256]{3,2,1,0:T(8,128)(2,1)S(1)}, bf16[8,4,256,256]{3,2,1,0:T(8,128)(2,1)}, u32[]{:S(2)}) copy-start(bf16[8,4,256,256]{3,2,1,0:T(8,128)(2,1)} %couple.7) | copy-start | bytes 12582916
  12.5 1.6 %copy-start.7 = (bf16[8,512,256]{2,1,0:T(8,128)(2,1)S(1)}, bf16[8,512,256]{2,1,0:T(8,128)(2,1)}, u32[]{:S(2)}) copy-start(bf16[8,512,256]{2,1,0:T(8,128)(2,1)} %copy-done.6) | copy-start | bytes 6291460
  14.1 0.7 collective-permute-start.11
  14.8 0.7 collective-permute-start.12
  15.5 2.2 %copy-start.3 = (bf16[8,4,256,256]{3,2,1,0:T(8,128)(2,1)S(1)}, bf16[8,4,256,256]{3,2,1,0:T(8,128)(2,1)}, u32[]{:S(2)}) copy-start(bf16[8,4,256,256]{3,2,1,0:T(8,128)(2,1)} %couple.7) | copy-start | bytes 12582916
  15.5 1.0 %collective-permute-start.13 = (f32[8,256]{1,0:T(8,128)S(1)}, f32[8,256]{1,0:T(8,128)S(1)}, u32[]{:S(2)}, u32[]{:S(2)}) collective-permute-start(f32[8,256]{1,0:T(8,128)S(1)} %step.18), channel_id=1, source_target_pairs={{192,224},{193,225},{194,226},{195,227},{196,228},{197,229},{198,2... | collective-permute-start | bytes 24584 | tf_op jit(solution)/shard_map/ppermute | solution.py:451
  16.5 6.0 %collective-permute-start.14 = (f32[8,256]{1,0:T(8,128)S(1)}, f32[8,256]{1,0:T(8,128)S(1)}, u32[]{:S(2)}, u32[]{:S(2)}) collective-permute-start(f32[8,256]{1,0:T(8,128)S(1)} %step.19._), channel_id=1, source_target_pairs={{224,192},{225,193},{226,194},{227,195},{228,196},{229,197},{230,1... | collective-permute-start | bytes 24584 | tf_op jit(solution)/shard_map/ppermute | solution.py:478
  22.6 0.7 collective-permute-start.15
  23.3 20.6 %copy-start.8 = (bf16[8,256,256]{2,1,0:T(8,128)(2,1)S(1)}, bf16[8,256,256]{2,1,0:T(8,128)(2,1)}, u32[]{:S(2)}) copy-start(bf16[8,256,256]{2,1,0:T(8,128)(2,1)} %skeleton.1) | copy-start | bytes 3145732
  23.3 0.8 collective-permute-start.16
  24.2 10.4 %collective-permute-start.17 = (f32[8,256]{1,0:T(8,128)S(1)}, f32[8,256]{1,0:T(8,128)S(1)}, u32[]{:S(2)}, u32[]{:S(2)}) collective-permute-start(f32[8,256]{1,0:T(8,128)S(1)} %step.22._), channel_id=1, source_target_pairs={{128,96},{129,97},{130,98},{131,99},{132,100},{133,101},{134,102},... | collective-permute-start | bytes 24584 | tf_op jit(solution)/shard_map/ppermute | solution.py:478
  25.5 16.7 %all-to-all-start.1 = ((f32[32,8,128]{2,1,0:T(8,128)}), f32[32,8,128]{2,1,0:T(8,128)S(1)}, u32[]{:S(2)}, u32[]{:S(2)}) async-start(f32[32,8,128]{2,1,0:T(8,128)} %announce.1), calls=%async_computation.1 | async-start | bytes 262144 | tf_op jit(solution)/shard_map/all_to_all | solution.py:490
  42.2 2.2 %copy-start.1 = (bf16[8,4,256,256]{3,2,1,0:T(8,128)(2,1)S(1)}, bf16[8,4,256,256]{3,2,1,0:T(8,128)(2,1)}, u32[]{:S(2)}) copy-start(bf16[8,4,256,256]{3,2,1,0:T(8,128)(2,1)} %pivots.7) | copy-start | bytes 12582916
  42.2 0.8 collective-permute-start.18
  43.1 5.5 %collective-permute-start.19 = (f32[8,256]{1,0:T(8,128)S(1)}, f32[8,256]{1,0:T(8,128)S(1)}, u32[]{:S(2)}, u32[]{:S(2)}) collective-permute-start(f32[8,256]{1,0:T(8,128)S(1)} %step.24), channel_id=1, source_target_pairs={{64,32},{65,33},{66,34},{67,35},{68,36},{69,37},{70,38},{71,39},{7... | collective-permute-start | bytes 24584 | tf_op jit(solution)/shard_map/ppermute | solution.py:478
  44.4 2.2 %copy-start.4 = (bf16[8,4,256,256]{3,2,1,0:T(8,128)(2,1)S(1)}, bf16[8,4,256,256]{3,2,1,0:T(8,128)(2,1)}, u32[]{:S(2)}) copy-start(bf16[8,4,256,256]{3,2,1,0:T(8,128)(2,1)} %couple.7) | copy-start | bytes 12582916
  46.6 22.6 %copy-start.5 = (bf16[8,4,256,256]{3,2,1,0:T(8,128)(2,1)S(1)}, bf16[8,4,256,256]{3,2,1,0:T(8,128)(2,1)}, u32[]{:S(2)}) copy-start(bf16[8,4,256,256]{3,2,1,0:T(8,128)(2,1)} %couple.7) | copy-start | bytes 12582916
  48.6 20.6 %collective-permute-start.20 = (f32[8,256]{1,0:T(8,128)S(1)}, f32[8,256]{1,0:T(8,128)S(1)}, u32[]{:S(2)}, u32[]{:S(2)}) collective-permute-start(f32[8,256]{1,0:T(8,128)S(1)} %step.25), channel_id=1, source_target_pairs={{32,0},{33,1},{34,2},{35,3},{36,4},{37,5},{38,6},{39,7},{40,8},{41... | collective-permute-start | bytes 24584 | tf_op jit(solution)/shard_map/ppermute | solution.py:478
  92.7 0.6 copy-start.10

commit v3 on v2

--- a/solution.py
+++ b/solution.py
@@ -128,7 +128,7 @@
     return values
 
 
-def transfer(source, pivots_far, couple_far, matrix, base, pivots, couple, kept, semaphores):
+def transfer(early, source, pivots_far, couple_far, _, matrix, base, pivots, couple, kept, semaphores):
     lines, columns = pivots.shape[:2]
     size = pivots.shape[2]
     here = lax.axis_index("down")
@@ -152,12 +152,14 @@
             store_pair(matrix, line, halves(value[:size]))
             base[pl.ds(line, 1), :] = value[size : size + 1]
 
-    @pl.when(here > 0)
+    active = here == 1 if early else here > 1
+
+    @pl.when(active)
     def _():
         for line in range(TOGETHER):
             fetch(line, lambda copy: copy.start())
 
-    @pl.when(jnp.logical_and(here > 0, here < last))
+    @pl.when(jnp.logical_and(active, here < last))
     def _():
         @pl.loop(0, lines, step=TOGETHER)
         def _(first):
@@ -165,7 +167,7 @@
             arrive(some, first)
             hand_over(some, forward_rows(source, pivots, couple, some))
 
-    @pl.when(here == last)
+    @pl.when(jnp.logical_and(active, here == last))
     def _():
         @pl.loop(0, lines, step=TOGETHER)
         def _(first):
@@ -450,11 +452,11 @@
     for hop in range(1, depth):
         arrived = lax.ppermute(sent, "down", [(hop - 1, hop)])
         arrivals.append(arrived)
-        if hop == 1:
+        if hop <= 2:
             matrix, base = call(
-                transfer,
+                functools.partial(transfer, hop == 1),
                 (stacked, vectors),
-                [IN_VMEM, IN_HBM, IN_HBM],
+                [IN_VMEM, IN_HBM, IN_HBM, ANYWHERE],
                 [
                     matrices,
                     matrices,
@@ -463,7 +465,7 @@
                 ],
                 name="transfer",
                 limit=49,
-            )(source, pivot_inverse, coupling)
+            )(source, pivot_inverse, coupling, coupling if hop == 1 else sent)
         if hop == 4:
             back = call(
                 reverse_transfer, stacked, [IN_VMEM, IN_VMEM, ANYWHERE], name="reverse_transfer"

time: 93.8 us -> 92.4 us (0.985)
  local copies, waits for them, and re-layouts: 7.87 us -> 4.95 us
  blocking collectives: 20 us -> 22.9 us
  waiting for transfers between devices: 27.4 us -> 25.7 us
    all_to_all x1, blocking collectives: 20 us -> 22.9 us  [spread_out(): moved = lax.all_to_all(packed.reshape(group, SLOTS, size), PLANE, 0, 0)]
    unnamed x36 -> x30, local copies, waits for them, and re-layouts: 7.6 us -> 4.68 us
    ppermute x7, waiting for transfers between devices: 19.4 us -> 17.7 us  [shards(): arrived = lax.ppermute(sent, 'down', [(hop, hop - 1)])]
  transfers between devices with their start and end apart: 15 -> 15, of which waited for: 3 -> 3; matrix products, arithmetic and copies ran while one was open for 0% -> 0% of each run, Pallas kernels for 7% -> 8%
where the time goes in v3:
time: 92.4 us; the launch traced here: 92 us
  waiting for transfers between devices  25.7 us (28%)
  blocking collectives  22.9 us (25%)
  starting transfers between devices  20.5 us (22%)
  Pallas kernels  15.6 us (17%)
  local copies, waits for them, and re-layouts  4.95 us (5%)
  between operations  2.14 us (2%)
    all_to_all x1, blocking collectives, spread_out(): moved = lax.all_to_all(packed.reshape(group, SLOTS, size), PLANE, 0, 0)  22.9 us
    ppermute x7, waiting for transfers between devices, shards(): arrived = lax.ppermute(sent, 'down', [(hop, hop - 1)])  17.7 us
    all_to_all x1, starting transfers between devices, shards(): everyone = lax.all_to_all(everyone, PLANE, 0, 0)  9.16 us
    all_to_all x1, waiting for transfers between devices, shards(): everyone = lax.all_to_all(everyone, PLANE, 0, 0)  7.61 us
    ppermute x7, starting transfers between devices, shards(): arrived = lax.ppermute(sent, 'down', [(hop, hop - 1)])  5.87 us
    ppermute x7, starting transfers between devices, shards(): arrived = lax.ppermute(sent, 'down', [(hop - 1, hop)])  5.5 us
    pallas_call x1, Pallas kernels, shards(): call(own_part, (every, vectors), [IN_VMEM] * 4 + [ANYWHERE], name='own_pa...  4.93 us
    pallas_call x1, Pallas kernels, shards(): call(first_sweep, vectors, [IN_HBM] * 3, [pltpu.VMEM(source.shape, F32),...  4.86 us
  transfers between devices with their start and end apart: 15, of which 3 were waited for; matrix products, arithmetic and copies ran while one was open for 0% of the time, Pallas kernels for 8%

profile of v3, /device:TPU:1, one launch (start us, length us, event | category | flops | bytes accessed | tf_op | source)
XLA Modules:
  0.0 92.0 jit_solution(6406369985185680554)
XLA Ops:
  0.6 4.9 %first_sweep.1 = f32[8,256]{1,0:T(8,128)} custom-call(f32[8,4,256]{2,1,0:T(4,128)} %source.5, bf16[8,4,256,256]{3,2,1,0:T(8,128)(2,1)} %pivots.7, bf16[8,4,256,256]{3,2,1,0:T(8,128)(2,1)} %couple.7), custom_call_target="tpu_custom_call" | custom-call | tf_op jit(solution)/shard_map/first_sweep/pallas_call | solution.py:436
  5.5 1.3 %collective-permute-start.7 = (f32[8,256]{1,0:T(8,128)}, f32[8,256]{1,0:T(8,128)S(1)}, u32[]{:S(2)}, u32[]{:S(2)}) collective-permute-start(f32[8,256]{1,0:T(8,128)} %first_sweep.1), channel_id=1, source_target_pairs={{0,32},{1,33},{2,34},{3,35},{4,36},{5,37},{6,38},{7,39},{8,40},{9,... | collective-permute-start | bytes 24584 | tf_op jit(solution)/shard_map/ppermute | solution.py:453
  7.1 0.2 transfer.2
  7.4 0.4 collective-permute-done.7.arrived
  7.8 0.6 collective-permute-start.8
  8.5 0.4 transfer.3
  8.9 0.8 collective-permute-start.9
  9.7 0.8 collective-permute-start.10
  10.7 1.4 %copy-done = bf16[8,4,256,256]{3,2,1,0:T(8,128)(2,1)S(1)} copy-done((bf16[8,4,256,256]{3,2,1,0:T(8,128)(2,1)S(1)}, bf16[8,4,256,256]{3,2,1,0:T(8,128)(2,1)}, u32[]{:S(2)}) %copy-start) | copy-done | bytes 4194328
  12.0 0.7 collective-permute-start.11
  12.7 0.7 collective-permute-start.12
  13.5 0.7 collective-permute-start.13
  14.2 0.7 collective-permute-start.14
  14.9 4.9 %own_part.1 = (f32[4,8,256]{2,1,0:T(8,128)S(1)}, f32[8,256]{1,0:T(8,128)S(1)}) custom-call(bf16[8,4,256,256]{3,2,1,0:T(8,128)(2,1)S(1)} %copy-done.2, bf16[8,4,256,256]{3,2,1,0:T(8,128)(2,1)S(1)} %copy-done, f32[8,4,256]{2,1,0:T(4,128)S(1)} %copy-done.6, f32[7,8,256]{2,1,0:T(8,128)S(1)} %constant_dynamic-update-slice_fusion.arrived, f32[8,256]{1,0:T(8,128)S(1)} %step.19._), custom_call_target="tpu_custom_call" | custom-call | tf_op jit(solution)/shard_map/own_part/pallas_call | solution.py:474
  19.8 0.7 collective-permute-start.15
  20.5 0.7 collective-permute-start.16
  21.3 0.8 collective-permute-start.17
  22.1 0.7 announce.1
  22.7 9.2 %all-to-all-start.1 = ((f32[32,8,128]{2,1,0:T(8,128)}), f32[32,8,128]{2,1,0:T(8,128)S(1)}, u32[]{:S(2)}, u32[]{:S(2)}) async-start(f32[32,8,128]{2,1,0:T(8,128)} %announce.1), calls=%async_computation.1 | async-start | bytes 262144 | tf_op jit(solution)/shard_map/all_to_all | solution.py:492
  31.9 7.6 %all-to-all-done.1._.everyone = f32[32,8,128]{2,1,0:T(8,128)S(1)} async-done(((f32[32,8,128]{2,1,0:T(8,128)}), f32[32,8,128]{2,1,0:T(8,128)S(1)}, u32[]{:S(2)}, u32[]{:S(2)}) %all-to-all-start.1) | async-done | bytes 131104 | tf_op jit(solution)/shard_map/all_to_all | solution.py:492
  39.5 1.0 %collective-permute-start.18 = (f32[8,256]{1,0:T(8,128)S(1)}, f32[8,256]{1,0:T(8,128)S(1)}, u32[]{:S(2)}, u32[]{:S(2)}) collective-permute-start(f32[8,256]{1,0:T(8,128)S(1)} %step.23), channel_id=1, source_target_pairs={{96,64},{97,65},{98,66},{99,67},{100,68},{101,69},{102,70},{103,71... | collective-permute-start | bytes 24584 | tf_op jit(solution)/shard_map/ppermute | solution.py:480
  40.6 0.8 collective-permute-start.19
  41.4 0.3 copy-done.1
  41.7 2.2 %copy-done.3 = bf16[8,4,256,256]{3,2,1,0:T(8,128)(2,1)S(1)} copy-done((bf16[8,4,256,256]{3,2,1,0:T(8,128)(2,1)S(1)}, bf16[8,4,256,256]{3,2,1,0:T(8,128)(2,1)}, u32[]{:S(2)}) %copy-start.3) | copy-done | bytes 4194328
  43.9 0.9 %plan_rows.1 = (f32[8,256]{1,0:T(8,128)S(1)}, s32[1,1]{1,0:T(1,128)}) custom-call(f32[32,8,128]{2,1,0:T(8,128)S(1)} %all-to-all-done.1._.everyone, bf16[8,4,256,256]{3,2,1,0:T(8,128)(2,1)S(1)} %copy-done.3, bf16[8,4,256,256]{3,2,1,0:T(8,128)(2,1)S(1)} %copy-done.1, bf16[8,256,256]{2,1,0:T(8,128)(2,1)S(1)} %copy-done.5, ...), custom_call_target="tpu_custom_call" | custom-call | tf_op jit(solution)/shard_map/plan_rows/pallas_call | solution.py:483
  45.9 1.3 %collective-permute-start.20 = (f32[8,256]{1,0:T(8,128)S(1)}, f32[8,256]{1,0:T(8,128)S(1)}, u32[]{:S(2)}, u32[]{:S(2)}) collective-permute-start(f32[8,256]{1,0:T(8,128)S(1)} %step.25), channel_id=1, source_target_pairs={{32,0},{33,1},{34,2},{35,3},{36,4},{37,5},{38,6},{39,7},{40,8},{41... | collective-permute-start | bytes 24584 | tf_op jit(solution)/shard_map/ppermute | solution.py:480
  47.2 17.7 %collective-permute-done.20 = f32[8,256]{1,0:T(8,128)S(1)} collective-permute-done((f32[8,256]{1,0:T(8,128)S(1)}, f32[8,256]{1,0:T(8,128)S(1)}, u32[]{:S(2)}, u32[]{:S(2)}) %collective-permute-start.20) | collective-permute-done | bytes 8224 | tf_op jit(solution)/shard_map/ppermute | solution.py:480
  64.9 3.3 %finish.1 = (f32[8,4,256]{2,1,0:T(4,128)}, f32[40,256]{1,0:T(8,128)S(1)}, f32[256,256]{1,0:T(8,128)S(1)}) custom-call(bf16[8,4,256,256]{3,2,1,0:T(8,128)(2,1)S(1)} %copy-done.4, bf16[8,4,256,256]{3,2,1,0:T(8,128)(2,1)S(1)} %copy-done.1, bf16[8,256,256]{2,1,0:T(8,128)(2,1)S(1)} %copy-done.5, f32[8,256]{1,0:T(8,128)S(1)} %broadcast_in_dim.14.codes, ...), custom_call_target="tpu_custom_call" | custom-call | tf_op jit(solution)/shard_map/finish/pallas_call | solution.py:496
  68.2 23.1 %conditional.1 = (f32[8,4,256]{2,1,0:T(4,128)S(1)}) conditional(s32[]{:T(128)} %bitcast.20, f32[40,256]{1,0:T(8,128)S(1)} %get-tuple-element.39, (f32[256,256]{1,0:T(8,128)S(1)}, f32[8,256]{1,0:T(8,128)S(1)}) %tuple.14), branch_computations={%region_1.2_spmd, %region_2.3_spmd} | conditional | flops 20480 | bytes 1868064 | solution.py:502
  68.2 22.9 %all_to_all.9 = f32[32,8,256]{2,1,0:T(8,128)S(1)} all-to-all(f32[32,8,256]{2,1,0:T(8,128)S(1)} %bitcast.42), channel_id=1, replica_groups=mesh['down'=8,'cross'=16,'elev'=2] {'cross','elev'}, dimensions={0} | all-to-all | bytes 524288 | tf_op jit(solution)/shard_map/cond/branch_1_fun/all_to_all | solution.py:430
  91.2 0.2 place_rows.1
  91.4 0.6 copy-done.7
  (66 shorter events, 0.8 us)
Async XLA Ops:
  0.6 6.5 %copy-start.6 = (f32[8,4,256]{2,1,0:T(4,128)S(1)}, f32[8,4,256]{2,1,0:T(4,128)}, u32[]{:S(2)}) copy-start(f32[8,4,256]{2,1,0:T(4,128)} %source.5) | copy-start | bytes 98308
  0.6 6.2 %copy-start.8 = (s32[8,4]{0,1:T(4,128)S(1)}, s32[8,4]{0,1:T(4,128)}, u32[]{:S(2)}) copy-start(s32[8,4]{0,1:T(4,128)} %param.11) | copy-start | bytes 388
  5.5 2.3 %collective-permute-start.7 = (f32[8,256]{1,0:T(8,128)}, f32[8,256]{1,0:T(8,128)S(1)}, u32[]{:S(2)}, u32[]{:S(2)}) collective-permute-start(f32[8,256]{1,0:T(8,128)} %first_sweep.1), channel_id=1, source_target_pairs={{0,32},{1,33},{2,34},{3,35},{4,36},{5,37},{6,38},{7,39},{8,40},{9,... | collective-permute-start | bytes 24584 | tf_op jit(solution)/shard_map/ppermute | solution.py:453
  7.8 1.0 %collective-permute-start.8 = (f32[8,256]{1,0:T(8,128)S(1)}, f32[8,256]{1,0:T(8,128)S(1)}, u32[]{:S(2)}, u32[]{:S(2)}) collective-permute-start(f32[8,256]{1,0:T(8,128)S(1)} %step.13._), channel_id=1, source_target_pairs={{32,64},{33,65},{34,66},{35,67},{36,68},{37,69},{38,70},{39,71},{4... | collective-permute-start | bytes 24584 | tf_op jit(solution)/shard_map/ppermute | solution.py:453
  8.5 2.2 %copy-start.2 = (bf16[8,4,256,256]{3,2,1,0:T(8,128)(2,1)S(1)}, bf16[8,4,256,256]{3,2,1,0:T(8,128)(2,1)}, u32[]{:S(2)}) copy-start(bf16[8,4,256,256]{3,2,1,0:T(8,128)(2,1)} %pivots.7) | copy-start | bytes 12582916
  8.9 3.2 %copy-start = (bf16[8,4,256,256]{3,2,1,0:T(8,128)(2,1)S(1)}, bf16[8,4,256,256]{3,2,1,0:T(8,128)(2,1)}, u32[]{:S(2)}) copy-start(bf16[8,4,256,256]{3,2,1,0:T(8,128)(2,1)} %couple.7) | copy-start | bytes 12582916
  8.9 0.8 collective-permute-start.9
  9.7 2.3 %collective-permute-start.10 = (f32[8,256]{1,0:T(8,128)S(1)}, f32[8,256]{1,0:T(8,128)S(1)}, u32[]{:S(2)}, u32[]{:S(2)}) collective-permute-start(f32[8,256]{1,0:T(8,128)S(1)} %step.15._), channel_id=1, source_target_pairs={{96,128},{97,129},{98,130},{99,131},{100,132},{101,133},{102,134},... | collective-permute-start | bytes 24584 | tf_op jit(solution)/shard_map/ppermute | solution.py:453
  12.0 0.7 collective-permute-start.11
  12.7 0.7 collective-permute-start.12
  13.5 0.7 collective-permute-start.13
  14.2 5.6 %collective-permute-start.14 = (f32[8,256]{1,0:T(8,128)S(1)}, f32[8,256]{1,0:T(8,128)S(1)}, u32[]{:S(2)}, u32[]{:S(2)}) collective-permute-start(f32[8,256]{1,0:T(8,128)S(1)} %step.19._), channel_id=1, source_target_pairs={{224,192},{225,193},{226,194},{227,195},{228,196},{229,197},{230,1... | collective-permute-start | bytes 24584 | tf_op jit(solution)/shard_map/ppermute | solution.py:480
  19.8 0.7 collective-permute-start.15
  20.5 0.7 collective-permute-start.16
  21.2 20.2 %copy-start.5 = (bf16[8,256,256]{2,1,0:T(8,128)(2,1)S(1)}, bf16[8,256,256]{2,1,0:T(8,128)(2,1)}, u32[]{:S(2)}) copy-start(bf16[8,256,256]{2,1,0:T(8,128)(2,1)} %skeleton.1) | copy-start | bytes 3145732
  21.3 10.6 %collective-permute-start.17 = (f32[8,256]{1,0:T(8,128)S(1)}, f32[8,256]{1,0:T(8,128)S(1)}, u32[]{:S(2)}, u32[]{:S(2)}) collective-permute-start(f32[8,256]{1,0:T(8,128)S(1)} %step.22._), channel_id=1, source_target_pairs={{128,96},{129,97},{130,98},{131,99},{132,100},{133,101},{134,102},... | collective-permute-start | bytes 24584 | tf_op jit(solution)/shard_map/ppermute | solution.py:480
  22.7 16.8 %all-to-all-start.1 = ((f32[32,8,128]{2,1,0:T(8,128)}), f32[32,8,128]{2,1,0:T(8,128)S(1)}, u32[]{:S(2)}, u32[]{:S(2)}) async-start(f32[32,8,128]{2,1,0:T(8,128)} %announce.1), calls=%async_computation.1 | async-start | bytes 262144 | tf_op jit(solution)/shard_map/all_to_all | solution.py:492
  39.5 2.2 %copy-start.1 = (bf16[8,4,256,256]{3,2,1,0:T(8,128)(2,1)S(1)}, bf16[8,4,256,256]{3,2,1,0:T(8,128)(2,1)}, u32[]{:S(2)}) copy-start(bf16[8,4,256,256]{3,2,1,0:T(8,128)(2,1)} %couple.7) | copy-start | bytes 12582916
  39.5 1.0 %collective-permute-start.18 = (f32[8,256]{1,0:T(8,128)S(1)}, f32[8,256]{1,0:T(8,128)S(1)}, u32[]{:S(2)}, u32[]{:S(2)}) collective-permute-start(f32[8,256]{1,0:T(8,128)S(1)} %step.23), channel_id=1, source_target_pairs={{96,64},{97,65},{98,66},{99,67},{100,68},{101,69},{102,70},{103,71... | collective-permute-start | bytes 24584 | tf_op jit(solution)/shard_map/ppermute | solution.py:480
  40.6 5.2 %collective-permute-start.19 = (f32[8,256]{1,0:T(8,128)S(1)}, f32[8,256]{1,0:T(8,128)S(1)}, u32[]{:S(2)}, u32[]{:S(2)}) collective-permute-start(f32[8,256]{1,0:T(8,128)S(1)} %step.24), channel_id=1, source_target_pairs={{64,32},{65,33},{66,34},{67,35},{68,36},{69,37},{70,38},{71,39},{7... | collective-permute-start | bytes 24584 | tf_op jit(solution)/shard_map/ppermute | solution.py:480
  41.7 2.2 %copy-start.3 = (bf16[8,4,256,256]{3,2,1,0:T(8,128)(2,1)S(1)}, bf16[8,4,256,256]{3,2,1,0:T(8,128)(2,1)}, u32[]{:S(2)}) copy-start(bf16[8,4,256,256]{3,2,1,0:T(8,128)(2,1)} %pivots.7) | copy-start | bytes 12582916
  43.9 21.0 %copy-start.4 = (bf16[8,4,256,256]{3,2,1,0:T(8,128)(2,1)S(1)}, bf16[8,4,256,256]{3,2,1,0:T(8,128)(2,1)}, u32[]{:S(2)}) copy-start(bf16[8,4,256,256]{3,2,1,0:T(8,128)(2,1)} %pivots.7) | copy-start | bytes 12582916
  45.9 19.0 %collective-permute-start.20 = (f32[8,256]{1,0:T(8,128)S(1)}, f32[8,256]{1,0:T(8,128)S(1)}, u32[]{:S(2)}, u32[]{:S(2)}) collective-permute-start(f32[8,256]{1,0:T(8,128)S(1)} %step.25), channel_id=1, source_target_pairs={{32,0},{33,1},{34,2},{35,3},{36,4},{37,5},{38,6},{39,7},{40,8},{41... | collective-permute-start | bytes 24584 | tf_op jit(solution)/shard_map/ppermute | solution.py:480
  91.4 0.6 copy-start.7
